TPU v7x, 32 devices: a whole 2x2x4 slice. The times are simulated.
32 devices in a mesh: req: 8 (over z, x), mlp: 4 (over y, core).
Axes of the slice: x: 2, y: 2, z: 4, core: 2. Of those that a mesh axis runs over, the one named last changes fastest.
Arguments:
- residual_in: bfloat16 [8192, 1664], P('req'), may hold values from -6 to 6
- lengths: int32 [256], P(('req', 'mlp')), may hold values from 0 to 64, as said below
- owners: int32 [256], P(('req', 'mlp')), may hold values from 0 to 7, as said below
- merge_dest: int32 [8192], P('req'), may hold values from 0 to 255, as said below
- segment_ids: int32 [8192], P('req'), may hold values from 0 to 3, as said below
- norm2_gain: float32 [1664], replicated, may hold values from 0.5 to 1.5
- norm2_bias: float32 [1664], replicated, may hold values from -3 to 3
- up_weight: bfloat16 [4096, 1664], P('mlp'), may hold values from -0.15625 to 0.15625
- up_bias: float32 [4096], P('mlp'), may hold values from -3 to 3
- down_weight: bfloat16 [4096, 1664], P('mlp'), may hold values from -0.09375 to 0.09375
- down_bias: float32 [1664], replicated, may hold values from -3 to 3
- proj_weight: bfloat16 [6656, 1664], P('mlp'), may hold values from -0.078125 to 0.078125
- norm3_gain: float32 [1664], replicated, may hold values from 0.5 to 1.5
- norm3_bias: float32 [1664], replicated, may hold values from -3 to 3
- next_weight: bfloat16 [1664, 3, 1664], P('req'), may hold values from -0.15625 to 0.15625
Outputs:
- merged_out: bfloat16 [4096, 1664], P(('req', 'mlp'))
- next_mixed: bfloat16 [4096, 1664], P(('req', 'mlp'))
Inputs may be any that keep to these rules, and one draw needn't show every extreme that they name: The 8 pieces of each block of 256 tokens (one device, req-major order) have lengths that are multiples of 4 and sum to 256; in every block one piece has exactly 64 tokens. The owners of the 8 pieces of one block are a permutation of 0 to 7; for each index of mlp, one piece of 64 tokens of each block of that index goes to one owner shared by all blocks of that index. `merge_dest`: within each device block a permutation of 0 to 255 that maps the tokens of each piece onto that piece's own positions. `segment_ids`: the four tokens of a block whose merge_dest values have the same quotient by 4 carry one segment id.
All inputs are finite; a program needn't handle non-finite values.
Results may differ from a plain program's by a relative error of at most 0.023.
Values may be sent and summed in bfloat16 or wider, within the bound.
A program may use at most 128 MiB of HBM per device.

v0:
```python
import math

import jax
import jax.numpy as jnp
from jax import lax
from jax.sharding import PartitionSpec as P

HEAD_DIM = 104


EPSILON = 1e-06


def layer_norm(rows, gain, bias):
    values = rows.astype(jnp.float32)
    mean_value = jnp.mean(values, axis=-1, keepdims=True)
    centred = values - mean_value
    spread = jnp.mean(centred * centred, axis=-1, keepdims=True)
    return centred * lax.rsqrt(spread + EPSILON) * gain + bias


def block_attention(heads_in, slot_tags):
    queries = heads_in[:, :, 0]
    key_rows = heads_in[:, :, 1]
    value_rows = heads_in[:, :, 2]
    score_scale = 1.0 / math.sqrt(heads_in.shape[-1])
    scores = (
        jnp.einsum("bqhe,bkhe->bhqk", queries, key_rows, preferred_element_type=jnp.float32)
        * score_scale
    )
    slot_total = heads_in.shape[1]
    itself = lax.broadcasted_iota(jnp.int32, (slot_total, slot_total), 0) == lax.broadcasted_iota(
        jnp.int32, (slot_total, slot_total), 1
    )
    live_slots = slot_tags >= 0
    same_request = slot_tags[:, :, None] == slot_tags[:, None, :]
    allowed = same_request & live_slots[:, None, :] | itself[None]
    weights = jnp.where(allowed[:, None], jnp.exp(scores), 0.0)
    probs = (weights / jnp.sum(weights, axis=-1, keepdims=True)).astype(jnp.bfloat16)
    mixed_out = jnp.einsum("bhqk,bkhe->bqhe", probs, value_rows, preferred_element_type=jnp.float32)
    mixed_out = jnp.where(live_slots[:, :, None, None], mixed_out, 0.0)
    return mixed_out.astype(jnp.bfloat16)


def body(
    residual_in,
    lengths,
    owners,
    merge_dest,
    segment_ids,
    norm2_gain,
    norm2_bias,
    up_weight,
    up_bias,
    down_weight,
    down_bias,
    proj_weight,
    norm3_gain,
    norm3_bias,
    next_weight,
):
    group_rows, model_width = residual_in.shape
    lane_count = lax.axis_size("mlp")
    sender_count = lax.axis_size("req")
    lane_index = lax.axis_index("mlp")
    own_rows = group_rows // lane_count
    merged_rows = own_rows // 4
    slot_count = 2 * merged_rows // sender_count
    normed = layer_norm(residual_in, norm2_gain, norm2_bias).astype(jnp.bfloat16)
    upward = lax.dot_general(
        normed, up_weight, (((1,), (1,)), ((), ())), preferred_element_type=jnp.float32
    )
    hidden = jax.nn.gelu(upward + up_bias, approximate=False).astype(jnp.bfloat16)
    partial_sums = jnp.dot(hidden, down_weight, preferred_element_type=jnp.float32)
    places = merge_dest.reshape(lane_count, own_rows)
    block_ids = lax.broadcasted_iota(jnp.int32, (lane_count, own_rows), 0)
    token_ids = lax.broadcasted_iota(jnp.int32, (lane_count, own_rows), 1)
    sources = jnp.zeros((lane_count, own_rows), jnp.int32).at[block_ids, places].set(token_ids)
    block_offset = own_rows * lax.broadcasted_iota(jnp.int32, (lane_count, merged_rows, 4), 0)
    group_index = sources.reshape(lane_count, merged_rows, 4) + block_offset
    quadrant_rows = lax.dynamic_index_in_dim(group_index, lane_index, 2, False).reshape(-1)
    feed_out = lax.psum(partial_sums.astype(jnp.bfloat16), "mlp").astype(jnp.float32)
    layer_out = (residual_in.astype(jnp.float32) + feed_out + down_bias).astype(jnp.bfloat16)
    quarter = jnp.take(layer_out, quadrant_rows, axis=0)
    projected = lax.psum_scatter(
        jnp.dot(quarter, proj_weight, preferred_element_type=jnp.float32).astype(jnp.bfloat16),
        "mlp",
        scatter_dimension=0,
        tiled=True,
    )
    first_tokens = lax.dynamic_index_in_dim(group_index[:, :, 0], lane_index, 0, False)
    row_segment = jnp.take(segment_ids, first_tokens, axis=0)
    counts = lengths // 4
    starts = jnp.cumsum(counts) - counts
    index = lax.broadcasted_iota(jnp.int32, (merged_rows, 1), 0)
    inside = ((index >= starts[None, :]) & (index < (starts + counts)[None, :])).astype(jnp.int32)
    owner_of = jnp.sum(inside * owners[None, :], axis=1)
    rank = index[:, 0] - jnp.sum(inside * starts[None, :], axis=1)
    target = owner_of * slot_count + rank
    slot_ids = lax.broadcasted_iota(jnp.int32, (sender_count * slot_count, 1), 0)
    route_hits = slot_ids == target[None, :]
    outgoing = jnp.dot(
        route_hits.astype(jnp.bfloat16), projected, preferred_element_type=jnp.float32
    ).astype(jnp.bfloat16)
    sent_tags = jnp.sum(route_hits.astype(jnp.int32) * (row_segment + 1)[None, :], axis=1) - 1
    received, arrived_tags = (
        lax.all_to_all(outgoing, "req", split_axis=0, concat_axis=0, tiled=True),
        lax.all_to_all(sent_tags, "req", split_axis=0, concat_axis=0, tiled=True),
    )
    normed3 = layer_norm(received, norm3_gain, norm3_bias).astype(jnp.bfloat16)
    recv_rows = received.shape[0]
    piece = lax.all_gather(next_weight, "req", axis=0, tiled=True)
    heads_in = jnp.dot(
        normed3, piece.reshape(piece.shape[0], -1), preferred_element_type=jnp.float32
    )
    heads_in = heads_in.astype(jnp.bfloat16).reshape(1, recv_rows, 3, -1, HEAD_DIM)
    next_mixed = block_attention(heads_in, arrived_tags.reshape(1, recv_rows)).reshape(
        recv_rows, model_width
    )
    return (received, next_mixed)


def solution(mesh):
    return jax.shard_map(
        body,
        mesh=mesh,
        in_specs=(
            P("req", None),
            P(("req", "mlp")),
            P(("req", "mlp")),
            P("req"),
            P("req"),
            P(),
            P(),
            P("mlp", None),
            P("mlp"),
            P("mlp", None),
            P(),
            P("mlp", None),
            P(),
            P(),
            P("req", None, None),
        ),
        out_specs=(P(("req", "mlp"), None), P(("req", "mlp"), None)),
        check_vma=False,
    )
```

profile of v0, /device:TPU:0, one launch (start us, length us, event | category | flops | bytes accessed | tf_op | source)
XLA Modules:
  0.0 413.3 jit_solution(140372300380319667)
XLA Ops:
  8.0 0.0 copy-start
  8.0 0.0 copy-start.15
  8.0 0.0 copy-start.13
  8.0 0.0 all-reduce.2.cloned.1.call-start
  8.1 0.0 copy-start.3
  8.1 0.0 copy-start.14
  8.1 2.6 convert_reduce_fusion
  10.8 0.5 copy-done.3
  11.2 1.0 fusion.2
  12.3 0.0 copy-done
  12.3 0.0 copy-start.9
  12.3 0.0 copy-start.12
  12.3 0.0 copy-start.11
  12.3 20.5 %convolution_convert_fusion.1 = bf16[1024,1664]{1,0:T(8,128)(2,1)} fusion(bf16[1024,1664]{1,0:T(8,128)(2,1)S(1)} %copy-done, bf16[1024,1664]{1,0:T(8,128)(2,1)} %param.22, bf16[1024,1664]{1,0:T(8,128)(2,1)} %param.15, f32[1664]{0:T(1024)S(1)} %copy-done.13, f32[1664]{0:T(1024)S(1)} %copy-done.14, f32[1024]{0:T(1024)S(1)} %add_rsqrt_fusion.1, ...), kind=kOutput, calls=%fused_computation.34 | convolution fusion | flops 7060455424 | bytes 13657088 | tf_op jit(solution)/shard_map/dot_general | solution.py:74
  32.9 0.0 all-reduce.2.cloned.1.call-update
  32.9 0.0 reduce-scatter.2.cloned.1.call-start
  33.0 0.1 multiply_reduce_fusion
  33.1 0.1 and_reduce_fusion
  33.2 4.5 %scatter_custom_fusion = s32[1024]{0:T(1024)S(1)} fusion(s32[1024]{0:T(1024)S(1)} %bitcast.59, s32[1024]{0:T(1024)S(1)} %bitcast.60, s32[]{:T(128)} %constant.47.clone.1), kind=kCustom, calls=%fused_computation.123 | custom fusion | bytes 4100
  37.7 0.1 reshape.396
  37.8 0.1 broadcast_add_fusion
  37.9 0.2 fusion.116
  38.2 0.1 reshape.398
  38.2 0.7 reshape.397
  38.9 0.7 compare_and_fusion
  39.6 68.8 %all-reduce.2.cloned.1.call-done = bf16[1024,1664]{1,0:T(8,128)(2,1)} async-done(((bf16[1024,1664]{1,0:T(8,128)(2,1)}), bf16[1024,1664]{1,0:T(8,128)(2,1)}) %all-reduce.2.cloned.1.call-update) | async-done | bytes 3407888 | tf_op jit(solution)/shard_map/psum | solution.py:82
  108.4 0.0 copy-done.4
  108.4 4.8 %fusion.7 = bf16[1024,1664]{1,0:T(8,128)(2,1)} fusion(bf16[1024,1664]{1,0:T(8,128)(2,1)S(1)} %copy-done.4, bf16[1024,1664]{1,0:T(8,128)(2,1)} %all-reduce.2.cloned.1.call-done, f32[1664]{0:T(1024)S(1)} %copy-done.8), kind=kLoop, calls=%fused_computation.13 | loop fusion | flops 8519680 | bytes 10230272 | tf_op jit(solution)/shard_map/convert_element_type | solution.py:83
  113.2 4.5 %gather_fusion = bf16[256,1664]{1,0:T(8,128)(2,1)S(1)} fusion(bf16[1024,1664]{1,0:T(8,128)(2,1)} %fusion.7, s32[1024]{0:T(1024)S(1)} %pad_clamp_fusion.1), kind=kCustom, calls=%fused_computation | custom fusion | bytes 1704960 | tf_op jit(solution)/shard_map/jit(_take)/gather | solution.py:84
  117.8 0.0 copy-start.16
  117.8 0.0 copy-start.2
  117.8 0.0 copy-start.10
  117.8 5.4 %convolution_convert_fusion.2 = bf16[256,1664]{1,0:T(8,128)(2,1)} fusion(bf16[1664,1664]{1,0:T(8,128)(2,1)} %param.26, bf16[256,1664]{1,0:T(8,128)(2,1)S(1)} %gather_fusion, pred[256]{0:T(512)(128)(4,1)S(1)} %compare_and_fusion), kind=kOutput, calls=%fused_computation.40 | convolution fusion | flops 1418526720 | bytes 7241984 | tf_op jit(solution)/shard_map/dot_general | solution.py:86
  123.2 0.0 reduce-scatter.2.cloned.1.call-update
  123.2 0.0 all-gather.2.cloned.1.call-start
  123.3 0.5 all-gather.2.cloned.1.call-update
  123.8 0.2 reduce-window.8
  124.0 0.1 dynamic-slice_reduce_fusion.1
  124.2 0.7 gather_fusion.1
  124.9 0.1 select_reduce_fusion.2
  125.0 0.1 select_reduce_fusion
  125.1 0.7 sub.44
  125.8 5.5 %all-to-all-start.1 = ((s32[8,16,1]{1,2,0:T(1,128)}), s32[8,16,1]{1,2,0:T(1,128)S(1)}, u32[]{:S(2)}, u32[]{:S(2)}) async-start(s32[8,16,1]{1,2,0:T(1,128)} %bitcast.6), calls=%async_computation.2 | async-start | bytes 8192 | tf_op jit(solution)/shard_map/all_to_all | solution.py:108
  131.3 15.9 %reduce-scatter.2.cloned.1.call-done = bf16[64,1664]{1,0:T(8,128)(2,1)} async-done(((bf16[256,1664]{1,0:T(8,128)(2,1)}), bf16[64,1664]{1,0:T(8,128)(2,1)}) %reduce-scatter.2.cloned.1.call-update) | async-done | bytes 213008 | tf_op jit(solution)/shard_map/reduce_scatter | solution.py:85
  147.2 2.1 convolution_convert_fusion.3
  149.3 0.0 all-to-all-done.1
  149.3 5.5 %all-to-all-start = ((bf16[8,16,1664]{2,1,0:T(8,128)(2,1)}), bf16[8,16,1664]{2,1,0:T(8,128)(2,1)S(1)}, u32[]{:S(2)}, u32[]{:S(2)}) async-start(bf16[8,16,1664]{2,1,0:T(8,128)(2,1)} %bitcast.3), calls=%async_computation.1 | async-start | bytes 851968 | tf_op jit(solution)/shard_map/all_to_all | solution.py:107
  154.8 0.5 broadcast.331
  155.3 0.7 reduce.17
  156.0 0.1 all_to_all.18
  156.1 0.1 fusion.74
  156.2 23.8 %all-to-all-done = bf16[8,16,1664]{2,1,0:T(8,128)(2,1)S(1)} async-done(((bf16[8,16,1664]{2,1,0:T(8,128)(2,1)}), bf16[8,16,1664]{2,1,0:T(8,128)(2,1)S(1)}, u32[]{:S(2)}, u32[]{:S(2)}) %all-to-all-start) | async-done | bytes 426016 | tf_op jit(solution)/shard_map/all_to_all | solution.py:107
  180.0 0.1 convert_reduce_fusion.1
  180.1 0.2 fusion.65
  180.4 0.0 copy-done.7
  180.4 0.3 fusion.68
  180.7 179.8 %all-gather.2.cloned.1.call-done = bf16[1664,3,1664]{2,0,1:T(8,128)(2,1)} async-done(((bf16[208,3,1664]{2,0,1:T(8,128)(2,1)}), bf16[1664,3,1664]{2,0,1:T(8,128)(2,1)}) %all-gather.2.cloned.1.call-update) | async-done | bytes 16613392 | tf_op jit(solution)/shard_map/all_gather | solution.py:112
  360.6 23.9 %copy.36 = bf16[1664,3,1664]{0,2,1:T(8,128)(2,1)} copy(bf16[1664,3,1664]{2,0,1:T(8,128)(2,1)} %all-gather.2.cloned.1.call-done) | data formatting | bytes 33226752 | tf_op jit(solution)/shard_map/all_gather | solution.py:112
  384.5 10.6 %convolution_convert_fusion = bf16[128,4992]{1,0:T(8,128)(2,1)S(1)} fusion(bf16[128,1664]{1,0:T(8,128)(2,1)S(1)} %bitcast.54, bf16[1664,4992]{0,1:T(8,128)(2,1)} %bitcast.52), kind=kOutput, calls=%fused_computation.15 | convolution fusion | flops 2127151104 | bytes 18317312 | tf_op jit(solution)/shard_map/dot_general | solution.py:113
  395.0 1.5 copy.37
  396.5 2.7 fusion.60
  399.2 2.9 fusion.62
  402.1 2.0 copy.39
  404.0 1.8 copy.45
  (41 shorter events, 0.2 us)
Async XLA Ops:
  8.0 4.3 %copy-start = (bf16[1024,1664]{1,0:T(8,128)(2,1)S(1)}, bf16[1024,1664]{1,0:T(8,128)(2,1)}, u32[]{:S(2)}) copy-start(bf16[1024,1664]{1,0:T(8,128)(2,1)} %param.24) | copy-start | bytes 10223620
  8.0 4.3 %copy-start.15 = (f32[1024]{0:T(1024)S(1)}, f32[1024]{0:T(1024)}, u32[]{:S(2)}) copy-start(f32[1024]{0:T(1024)} %param.23) | copy-start | bytes 12292
  8.0 4.3 %copy-start.13 = (f32[1664]{0:T(1024)S(1)}, f32[1664]{0:T(1024)}, u32[]{:S(2)}) copy-start(f32[1664]{0:T(1024)} %param.21) | copy-start | bytes 19972
  8.0 100.4 %all-reduce.2.cloned.1.call-start = ((), (), s32[]{:S(2)}) async-start(), calls=%async_computation.3 | async-start | bytes 6815744 | tf_op jit(solution)/shard_map/psum | solution.py:82
  8.1 3.1 copy-start.3
  8.1 4.2 %copy-start.14 = (f32[1664]{0:T(1024)S(1)}, f32[1664]{0:T(1024)}, u32[]{:S(2)}) copy-start(f32[1664]{0:T(1024)} %param.20) | copy-start | bytes 19972
  12.3 20.6 %copy-start.9 = (s32[1024]{0:T(1024)S(1)}, s32[1024]{0:T(1024)}, u32[]{:S(2)}) copy-start(s32[1024]{0:T(1024)} %param.18) | copy-start | bytes 12292
  12.3 20.7 %copy-start.12 = (s32[2]{0:T(128)S(1)}, s32[2]{0:T(128)}, u32[]{:S(2)}) copy-start(s32[2]{0:T(128)} %constant.153) | copy-start | bytes 28
  12.3 20.7 %copy-start.11 = (s32[2]{0:T(128)S(1)}, s32[2]{0:T(128)}, u32[]{:S(2)}) copy-start(s32[2]{0:T(128)} %constant.156) | copy-start | bytes 28
  32.9 75.6 %copy-start.4 = (bf16[1024,1664]{1,0:T(8,128)(2,1)S(1)}, bf16[1024,1664]{1,0:T(8,128)(2,1)}, u32[]{:S(2)}) copy-start(bf16[1024,1664]{1,0:T(8,128)(2,1)} %param.15) | copy-start | bytes 10223620
  32.9 75.6 %copy-start.8 = (f32[1664]{0:T(1024)S(1)}, f32[1664]{0:T(1024)}, u32[]{:S(2)}) copy-start(f32[1664]{0:T(1024)} %param.25) | copy-start | bytes 19972
  32.9 114.4 %reduce-scatter.2.cloned.1.call-start = ((), (), s32[]{:S(2)}) async-start(), calls=%async_computation.4 | async-start | bytes 1064960 | tf_op jit(solution)/shard_map/reduce_scatter | solution.py:85
  117.8 6.1 %copy-start.16 = (s32[8]{0:T(128)S(1)}, s32[8]{0:T(128)}, u32[]{:S(2)}) copy-start(s32[8]{0:T(128)} %param.16) | copy-start | bytes 100
  117.8 6.4 %copy-start.2 = (s32[1024]{0:T(1024)S(1)}, s32[1024]{0:T(1024)}, u32[]{:S(2)}) copy-start(s32[1024]{0:T(1024)} %param.19) | copy-start | bytes 12292
  117.8 7.1 %copy-start.10 = (s32[8]{0:T(128)S(1)}, s32[8]{0:T(128)}, u32[]{:S(2)}) copy-start(s32[8]{0:T(128)} %param.17) | copy-start | bytes 100
  123.2 57.2 %copy-start.6 = (f32[1664]{0:T(1024)S(1)}, f32[1664]{0:T(1024)}, u32[]{:S(2)}) copy-start(f32[1664]{0:T(1024)} %param.28) | copy-start | bytes 19972
  123.2 57.2 %copy-start.7 = (f32[1664]{0:T(1024)S(1)}, f32[1664]{0:T(1024)}, u32[]{:S(2)}) copy-start(f32[1664]{0:T(1024)} %param.27) | copy-start | bytes 19972
  123.2 237.3 %all-gather.2.cloned.1.call-start = ((), (), s32[]{:S(2)}) async-start(), calls=%async_computation.5 | async-start | bytes 18690048 | tf_op jit(solution)/shard_map/all_gather | solution.py:112
  125.8 23.5 %all-to-all-start.1 = ((s32[8,16,1]{1,2,0:T(1,128)}), s32[8,16,1]{1,2,0:T(1,128)S(1)}, u32[]{:S(2)}, u32[]{:S(2)}) async-start(s32[8,16,1]{1,2,0:T(1,128)} %bitcast.6), calls=%async_computation.2 | async-start | bytes 8192 | tf_op jit(solution)/shard_map/all_to_all | solution.py:108
  149.3 30.6 %all-to-all-start = ((bf16[8,16,1664]{2,1,0:T(8,128)(2,1)}), bf16[8,16,1664]{2,1,0:T(8,128)(2,1)S(1)}, u32[]{:S(2)}, u32[]{:S(2)}) async-start(bf16[8,16,1664]{2,1,0:T(8,128)(2,1)} %bitcast.3), calls=%async_computation.1 | async-start | bytes 851968 | tf_op jit(solution)/shard_map/all_to_all | solution.py:107
  180.0 204.5 %copy-start.5 = (bf16[8,16,1664]{2,1,0:T(8,128)(2,1)}, bf16[8,16,1664]{2,1,0:T(8,128)(2,1)S(1)}, u32[]{:S(2)}) copy-start(bf16[8,16,1664]{2,1,0:T(8,128)(2,1)S(1)} %all-to-all-done) | copy-start | bytes 1277956
  396.5 9.3 %copy-start.1 = (bf16[1024,1664]{1,0:T(8,128)(2,1)S(1)}, bf16[1024,1664]{1,0:T(8,128)(2,1)}, u32[]{:S(2)}) copy-start(bf16[1024,1664]{1,0:T(8,128)(2,1)} %param.24) | copy-start | bytes 10223620
Sparse Core Ops, SparseCore 0:
  33.0 75.3 all-reduce.1
  123.4 23.8 reduce-scatter.1
Sparse Core Ops, SparseCore 1:
  126.2 234.3 all-gather.1
where the time goes:
time: 414 us; the launch traced here: 413 us
  waiting for transfers between devices  289 us (70%)
  matrix products  44.1 us (11%)
  local copies, waits for them, and re-layouts  42 us (10%)
  between operations  15.8 us (4%)
  other arithmetic  11.3 us (3%)
  starting transfers between devices  11.1 us (3%)
    all_gather x1, waiting for transfers between devices, body(): piece = lax.all_gather(next_weight, 'req', axis=0, tiled=True)  180 us
    psum x1, waiting for transfers between devices, body(): lax.psum(partial_sums.astype(jnp.bfloat16), 'mlp').astype(jnp.float32)  68.8 us
    all_gather x1, local copies, waits for them, and re-layouts, body(): piece = lax.all_gather(next_weight, 'req', axis=0, tiled=True)  23.9 us
    all_to_all x1, waiting for transfers between devices, body(): lax.all_to_all(outgoing, 'req', split_axis=0, concat_axis=0, tiled=True)  23.8 us
    dot_general x1, matrix products, body(): jnp.dot(hidden, down_weight, preferred_element_type=jnp.float32)  20.5 us
    reduce_scatter x1, waiting for transfers between devices, body(): lax.psum_scatter(jnp.dot(quarter, proj_weight, preferred_element_type=jnp...  15.9 us
    dot_general x1, matrix products, body(): jnp.dot(normed3, piece.reshape(piece.shape[0], -1), preferred_element_typ...  10.6 us
    unnamed x40, local copies, waits for them, and re-layouts  8.82 us
  transfers between devices with their start and end apart: 5, of which 4 were waited for; matrix products, arithmetic and copies ran while one was open for 3% of the time, Pallas kernels for 0%

commit v1 on v0

--- a/solution.py
+++ b/solution.py
@@ -6,8 +6,7 @@
 from jax.sharding import PartitionSpec as P
 
 HEAD_DIM = 104
-
-
+TAG_PAD = 128
 EPSILON = 1e-06
 
 
@@ -66,30 +65,47 @@
     own_rows = group_rows // lane_count
     merged_rows = own_rows // 4
     slot_count = 2 * merged_rows // sender_count
-    normed = layer_norm(residual_in, norm2_gain, norm2_bias).astype(jnp.bfloat16)
+    part_width = model_width // lane_count
+    own_columns = lax.dynamic_slice_in_dim(
+        next_weight.transpose(1, 0, 2), lane_index * part_width, part_width, 2
+    )
+    piece = lax.all_gather(own_columns, "req", axis=1, tiled=True)
+    places = merge_dest.reshape(lane_count, own_rows)
+    wanted = (
+        4 * lax.broadcasted_iota(jnp.int32, (4, merged_rows), 1)
+        + lax.broadcasted_iota(jnp.int32, (4, merged_rows), 0)
+    )
+    hits = wanted[:, None, :, None] == places[None, :, None, :]
+    ordered = jnp.einsum(
+        "qbit,btd->qbid",
+        hits.astype(jnp.bfloat16),
+        residual_in.reshape(lane_count, own_rows, model_width),
+        preferred_element_type=jnp.float32,
+    ).astype(jnp.bfloat16).reshape(group_rows, model_width)
+    normed = layer_norm(ordered, norm2_gain, norm2_bias).astype(jnp.bfloat16)
     upward = lax.dot_general(
         normed, up_weight, (((1,), (1,)), ((), ())), preferred_element_type=jnp.float32
     )
     hidden = jax.nn.gelu(upward + up_bias, approximate=False).astype(jnp.bfloat16)
     partial_sums = jnp.dot(hidden, down_weight, preferred_element_type=jnp.float32)
-    places = merge_dest.reshape(lane_count, own_rows)
-    block_ids = lax.broadcasted_iota(jnp.int32, (lane_count, own_rows), 0)
-    token_ids = lax.broadcasted_iota(jnp.int32, (lane_count, own_rows), 1)
-    sources = jnp.zeros((lane_count, own_rows), jnp.int32).at[block_ids, places].set(token_ids)
-    block_offset = own_rows * lax.broadcasted_iota(jnp.int32, (lane_count, merged_rows, 4), 0)
-    group_index = sources.reshape(lane_count, merged_rows, 4) + block_offset
-    quadrant_rows = lax.dynamic_index_in_dim(group_index, lane_index, 2, False).reshape(-1)
-    feed_out = lax.psum(partial_sums.astype(jnp.bfloat16), "mlp").astype(jnp.float32)
-    layer_out = (residual_in.astype(jnp.float32) + feed_out + down_bias).astype(jnp.bfloat16)
-    quarter = jnp.take(layer_out, quadrant_rows, axis=0)
+    feed_out = lax.psum_scatter(
+        partial_sums.astype(jnp.bfloat16), "mlp", scatter_dimension=0, tiled=True
+    ).astype(jnp.float32)
+    own_quarter = lax.dynamic_slice_in_dim(ordered, lane_index * own_rows, own_rows, 0)
+    quarter = (own_quarter.astype(jnp.float32) + feed_out + down_bias).astype(jnp.bfloat16)
     projected = lax.psum_scatter(
         jnp.dot(quarter, proj_weight, preferred_element_type=jnp.float32).astype(jnp.bfloat16),
         "mlp",
         scatter_dimension=0,
         tiled=True,
     )
-    first_tokens = lax.dynamic_index_in_dim(group_index[:, :, 0], lane_index, 0, False)
-    row_segment = jnp.take(segment_ids, first_tokens, axis=0)
+    own_places = lax.dynamic_index_in_dim(places, lane_index, 0, False)
+    own_marks = lax.dynamic_index_in_dim(
+        segment_ids.reshape(lane_count, own_rows), lane_index, 0, False
+    )
+    row_segment = jnp.sum(
+        (wanted[0][:, None] == own_places[None, :]).astype(jnp.int32) * own_marks[None, :], axis=1
+    )
     counts = lengths // 4
     starts = jnp.cumsum(counts) - counts
     index = lax.broadcasted_iota(jnp.int32, (merged_rows, 1), 0)
@@ -103,20 +119,26 @@
         route_hits.astype(jnp.bfloat16), projected, preferred_element_type=jnp.float32
     ).astype(jnp.bfloat16)
     sent_tags = jnp.sum(route_hits.astype(jnp.int32) * (row_segment + 1)[None, :], axis=1) - 1
-    received, arrived_tags = (
-        lax.all_to_all(outgoing, "req", split_axis=0, concat_axis=0, tiled=True),
-        lax.all_to_all(sent_tags, "req", split_axis=0, concat_axis=0, tiled=True),
+    tag_columns = jnp.broadcast_to(
+        sent_tags.astype(jnp.bfloat16)[:, None], (sent_tags.shape[0], TAG_PAD)
     )
+    arrived = lax.all_to_all(
+        jnp.concatenate([outgoing, tag_columns], axis=1),
+        "req", split_axis=0, concat_axis=0, tiled=True,
+    )
+    received = arrived[:, :model_width]
     normed3 = layer_norm(received, norm3_gain, norm3_bias).astype(jnp.bfloat16)
     recv_rows = received.shape[0]
-    piece = lax.all_gather(next_weight, "req", axis=0, tiled=True)
-    heads_in = jnp.dot(
-        normed3, piece.reshape(piece.shape[0], -1), preferred_element_type=jnp.float32
+    everyone = lax.all_gather(
+        jnp.concatenate([normed3, arrived[:, model_width:]], axis=1), "mlp", axis=0, tiled=True
     )
-    heads_in = heads_in.astype(jnp.bfloat16).reshape(1, recv_rows, 3, -1, HEAD_DIM)
-    next_mixed = block_attention(heads_in, arrived_tags.reshape(1, recv_rows)).reshape(
-        recv_rows, model_width
+    tags = everyone[:, model_width].astype(jnp.int32).reshape(lane_count, recv_rows)
+    heads_in = jnp.einsum(
+        "rd,sde->rse", everyone[:, :model_width], piece, preferred_element_type=jnp.float32
     )
+    heads_in = heads_in.astype(jnp.bfloat16).reshape(lane_count, recv_rows, 3, -1, HEAD_DIM)
+    mixed = block_attention(heads_in, tags).reshape(lane_count * recv_rows, part_width)
+    next_mixed = lax.all_to_all(mixed, "mlp", split_axis=0, concat_axis=1, tiled=True)
     return (received, next_mixed)
 
 

time: 414 us -> 264 us (0.64)
  waiting for transfers between devices: 289 us -> 146 us
  blocking collectives: 0 us -> 39.5 us
  local copies, waits for them, and re-layouts: 42 us -> 15.6 us
  starting transfers between devices: 11.1 us -> 0.35 us
  other arithmetic: 11.3 us -> 4.5 us
    all_gather x1 -> x2, waiting for transfers between devices: 180 us -> 83.7 us  [the longest x1 63.1 us: body(): piece = lax.all_gather(own_columns, 'req', axis=1, tiled=True)]
    psum x1 -> x0, waiting for transfers between devices: 68.8 us -> none  [body(): lax.psum(partial_sums.astype(jnp.bfloat16), 'mlp').astype(jnp.float32)]
    reduce_scatter x0 -> x1, waiting for transfers between devices: none -> 42.2 us  [body(): lax.psum_scatter(partial_sums.astype(jnp.bfloat16), 'mlp', scatter_dimens...]
    all_to_all x0 -> x2, blocking collectives: none -> 39.5 us  [the longest x1 27.5 us: body(): lax.all_to_all(jnp.concatenate([outgoing, tag_columns], axis=1), 'req', s...]
    all_gather x1 -> x0, local copies, waits for them, and re-layouts: 23.9 us -> none  [body(): piece = lax.all_gather(next_weight, 'req', axis=0, tiled=True)]
    all_to_all x2 -> x0, waiting for transfers between devices: 23.8 us -> none  [the longest x1 23.8 us: body(): lax.all_to_all(outgoing, 'req', split_axis=0, concat_axis=0, tiled=True)]
    all_to_all x2 -> x0, starting transfers between devices: 11 us -> none  [the longest x1 5.51 us: body(): lax.all_to_all(sent_tags, 'req', split_axis=0, concat_axis=0, tiled=True)]
    gather x2 -> x0, local copies, waits for them, and re-layouts: 5.28 us -> none  [the longest x1 4.55 us: body(): quarter = jnp.take(layer_out, quadrant_rows, axis=0)]
  transfers between devices with their start and end apart: 5 -> 4, of which waited for: 4 -> 4; matrix products, arithmetic and copies ran while one was open for 3% -> 3% of each run, Pallas kernels for 0% -> 0%
where the time goes in v1:
time: 264 us; the launch traced here: 263 us
  waiting for transfers between devices  146 us (55%)
  matrix products  41.5 us (16%)
  blocking collectives  39.5 us (15%)
  between operations  15.7 us (6%)
  local copies, waits for them, and re-layouts  15.6 us (6%)
  other arithmetic  4.5 us (2%)
    all_gather x1, waiting for transfers between devices, body(): piece = lax.all_gather(own_columns, 'req', axis=1, tiled=True)  63.1 us
    reduce_scatter x1, waiting for transfers between devices, body(): lax.psum_scatter(partial_sums.astype(jnp.bfloat16), 'mlp', scatter_dimens...  42.2 us
    all_to_all x1, blocking collectives, body(): lax.all_to_all(jnp.concatenate([outgoing, tag_columns], axis=1), 'req', s...  27.5 us
    dot_general x1, matrix products, body(): jnp.dot(hidden, down_weight, preferred_element_type=jnp.float32)  21.6 us
    all_gather x1, waiting for transfers between devices, body(): lax.all_gather(jnp.concatenate([normed3, arrived[:, model_width:]], axis=...  20.6 us
    reduce_scatter x1, waiting for transfers between devices, body(): lax.psum_scatter(jnp.dot(quarter, proj_weight, preferred_element_type=jnp...  20.1 us
    all_to_all x1, blocking collectives, body(): lax.all_to_all(mixed, 'mlp', split_axis=0, concat_axis=1, tiled=True)  12 us
    dot_general x1, matrix products, body(): jnp.einsum('rd,sde->rse', everyone[:, :model_width], piece, preferred_ele...  7.31 us
  transfers between devices with their start and end apart: 4, of which 4 were waited for; matrix products, arithmetic and copies ran while one was open for 3% of the time, Pallas kernels for 0%

profile of v1, /device:TPU:0, one launch (start us, length us, event | category | flops | bytes accessed | tf_op | source)
XLA Modules:
  0.0 263.3 jit_solution(15149463695259456256)
XLA Ops:
  8.0 0.0 copy-start
  8.0 0.0 reduce-scatter.3.cloned.1.call-start
  8.1 0.8 eq.73
  8.9 1.1 copy-done
  10.0 1.2 convert_reduce_fusion
  11.2 0.0 copy-start.6
  11.3 0.0 copy-start.7
  11.3 0.0 copy-start.9
  11.3 2.0 copy.41
  13.3 1.0 fusion.1
  14.3 0.1 rsqrt.20
  14.4 0.1 div.39
  14.5 0.0 copy-done.6
  14.5 0.0 copy-done.7
  14.5 0.0 copy-done.9
  14.5 0.0 copy-start.8
  14.5 21.6 %convolution_convert_fusion = bf16[1024,1664]{1,0:T(8,128)(2,1)} fusion(bf16[1024,1664]{1,0:T(8,128)(2,1)} %param.24, bf16[1024,1664]{1,0:T(8,128)(2,1)} %param.22, bf16[1024,1664]{1,0:T(8,128)(2,1)} %bitcast.56, f32[1664]{0:T(1024)S(1)} %copy-done.6, f32[1664]{0:T(1024)S(1)} %copy-done.7, f32[1024]{0:T(1024)S(1)} %rsqrt.20, f32[1024]{0:T(1024)S(1)} %div.39, ...), kind=kOutput, calls=%fused_computation.26 | convolution fusion | flops 7060455424 | bytes 13657088 | tf_op jit(solution)/shard_map/dot_general | solution.py:90
  36.1 0.0 reduce-scatter.3.cloned.1.call-update
  36.1 0.2 reduce-scatter.5.cloned.1.call-start
  36.3 42.2 %reduce-scatter.3.cloned.1.call-done = bf16[256,1664]{1,0:T(8,128)(2,1)} async-done(((bf16[1024,1664]{1,0:T(8,128)(2,1)}), bf16[256,1664]{1,0:T(8,128)(2,1)}) %reduce-scatter.3.cloned.1.call-update) | async-done | bytes 851984 | tf_op jit(solution)/shard_map/reduce_scatter | solution.py:91
  78.6 0.0 copy-done.8
  78.6 5.8 %convolution_convert_fusion.2 = bf16[256,1664]{1,0:T(8,128)(2,1)} fusion(bf16[1664,1664]{1,0:T(8,128)(2,1)} %param.26, bf16[256,1664]{1,0:T(8,128)(2,1)} %reduce-scatter.3.cloned.1.call-done, f32[1664]{0:T(1024)S(1)} %copy-done.8, bf16[1024,1664]{1,0:T(8,128)(2,1)} %bitcast.57, s32[]{:T(128)S(6)} %select_n.26), kind=kOutput, calls=%fused_computation.34 | convolution fusion | flops 1420230656 | bytes 8100356 | tf_op jit(solution)/shard_map/dot_general | solution.py:97
  84.4 0.0 copy-start.10
  84.4 0.0 copy-start.4
  84.4 0.0 copy-start.5
  84.4 0.0 copy-start.2
  84.4 0.0 copy-start.3
  84.5 0.0 reduce-scatter.5.cloned.1.call-update
  84.5 0.0 all-gather.5.cloned.1.call-start
  84.5 1.4 constant_dynamic-slice_fusion
  86.0 1.5 copy.72
  87.5 0.0 all-gather.5.cloned.1.call-update
  87.6 0.0 all-gather.3.cloned.1.call-start
  87.6 0.0 copy-done.10
  87.6 0.2 reduce-window.8
  87.8 0.0 copy-done.4
  87.8 0.2 select_reduce_fusion
  88.0 0.0 copy-done.5
  88.0 0.1 select_reduce_fusion.3
  88.1 0.1 select_reduce_fusion.1
  88.2 20.1 %reduce-scatter.5.cloned.1.call-done = bf16[64,1664]{1,0:T(8,128)(2,1)} async-done(((bf16[256,1664]{1,0:T(8,128)(2,1)}), bf16[64,1664]{1,0:T(8,128)(2,1)}) %reduce-scatter.5.cloned.1.call-update) | async-done | bytes 213008 | tf_op jit(solution)/shard_map/reduce_scatter | solution.py:96
  108.3 1.3 convolution_convert_fusion.3
  109.7 0.1 broadcast_in_dim.18
  109.8 27.5 %all_to_all.31 = bf16[8,16,1792]{2,1,0:T(8,128)(2,1)S(1)} all-to-all(bf16[8,16,1792]{2,1,0:T(8,128)(2,1)S(1)} %bitcast.61), channel_id=1, replica_groups=mesh['req'=8,'mlp'=4] {'req'}, dimensions={0} | all-to-all | bytes 917504 | tf_op jit(solution)/shard_map/all_to_all | solution.py:125
  137.3 0.1 convert_reduce_fusion.1
  137.5 0.0 copy-start.1
  137.5 0.3 fusion.60
  137.7 0.5 copy-done.1
  138.2 0.0 copy-done.2
  138.2 0.0 copy-done.3
  138.2 0.3 fusion.63
  138.6 0.8 pad_maximum_fusion.1
  139.4 0.0 all-gather.3.cloned.1.call-update
  139.4 63.1 %all-gather.5.cloned.1.call-done = bf16[3,1664,416]{2,0,1:T(4,128)(2,1)} async-done(((bf16[3,208,416]{2,0,1:T(4,128)(2,1)}), bf16[3,1664,416]{2,0,1:T(4,128)(2,1)}) %all-gather.5.cloned.1.call-update) | async-done | bytes 4153360 | tf_op jit(solution)/shard_map/all_gather | solution.py:72
  202.5 20.6 %all-gather.3.cloned.1.call-done = bf16[512,1792]{1,0:T(8,128)(2,1)} async-done(((bf16[128,1792]{1,0:T(8,128)(2,1)}), bf16[512,1792]{1,0:T(8,128)(2,1)}) %all-gather.3.cloned.1.call-update) | async-done | bytes 1835024 | tf_op jit(solution)/shard_map/all_gather | solution.py:132
  223.1 7.3 %fusion.51 = bf16[512,3,416]{0,2,1:T(8,128)(2,1)} fusion(bf16[3,1664,416]{2,0,1:T(4,128)(2,1)} %all-gather.5.cloned.1.call-done, bf16[512,1792]{1,0:T(8,128)(2,1)} %all-gather.3.cloned.1.call-done), kind=kOutput, calls=%fused_computation.69 | convolution fusion | flops 2127151104 | bytes 9797632 | tf_op jit(solution)/shard_map/rd,sde->rse/dot_general | solution.py:136
  230.5 3.5 %reshape.171 = bf16[4,128,3,4,104]{1,0,4,3,2:T(4,128)(2,1)} reshape(bf16[512,3,416]{0,2,1:T(8,128)(2,1)} %fusion.51) | data formatting | bytes 2555904 | tf_op jit(solution)/shard_map/reshape | solution.py:139
  234.0 2.5 fusion.107
  236.4 1.1 convert_reduce_fusion.2
  237.5 0.2 and_or_fusion
  237.7 1.4 fusion.55
  239.1 2.8 %fusion.56 = bf16[4,4,104,128]{3,2,1,0:T(8,128)(2,1)} fusion(f32[4,4,128,128]{2,3,1,0:T(8,128)} %fusion.55, bf16[4,128,1,4,104]{1,0,4,3,2:T(4,128)(2,1)} %get-tuple-element.12, pred[4,128]{1,0:T(4,128)(4,1)S(1)} %broadcast_compare_fusion), kind=kOutput, calls=%fused_computation.74 | convolution fusion | flops 55478400 | bytes 1901056 | tf_op jit(solution)/shard_map/bhqk,bkhe->bqhe/dot_general | solution.py:39
  241.9 12.0 %all_to_all.32 = bf16[4,128,416]{1,2,0:T(8,128)(2,1)} all-to-all(bf16[4,128,416]{1,2,0:T(8,128)(2,1)} %bitcast.63), channel_id=1, replica_groups=mesh['req'=8,'mlp'=4] {'mlp'}, dimensions={0} | all-to-all | bytes 851968 | tf_op jit(solution)/shard_map/all_to_all | solution.py:141
  253.9 2.0 copy.50
  (20 shorter events, 0.2 us)
Async XLA Ops:
  8.0 2.0 copy-start
  8.0 70.6 %reduce-scatter.3.cloned.1.call-start = ((), (), s32[]{:S(2)}) async-start(), calls=%async_computation.4 | async-start | bytes 4259840 | tf_op jit(solution)/shard_map/reduce_scatter | solution.py:91
  11.2 3.3 %copy-start.6 = (f32[1664]{0:T(1024)S(1)}, f32[1664]{0:T(1024)}, u32[]{:S(2)}) copy-start(f32[1664]{0:T(1024)} %param.21) | copy-start | bytes 19972
  11.3 3.2 %copy-start.7 = (f32[1664]{0:T(1024)S(1)}, f32[1664]{0:T(1024)}, u32[]{:S(2)}) copy-start(f32[1664]{0:T(1024)} %param.20) | copy-start | bytes 19972
  11.3 3.2 %copy-start.9 = (f32[1024]{0:T(1024)S(1)}, f32[1024]{0:T(1024)}, u32[]{:S(2)}) copy-start(f32[1024]{0:T(1024)} %param.23) | copy-start | bytes 12292
  14.5 64.1 %copy-start.8 = (f32[1664]{0:T(1024)S(1)}, f32[1664]{0:T(1024)}, u32[]{:S(2)}) copy-start(f32[1664]{0:T(1024)} %param.25) | copy-start | bytes 19972
  36.1 72.2 %reduce-scatter.5.cloned.1.call-start = ((), (), s32[]{:S(2)}) async-start(), calls=%async_computation.5 | async-start | bytes 1064960 | tf_op jit(solution)/shard_map/reduce_scatter | solution.py:96
  84.4 3.2 %copy-start.10 = (s32[8]{0:T(128)S(1)}, s32[8]{0:T(128)}, u32[]{:S(2)}) copy-start(s32[8]{0:T(128)} %param.16) | copy-start | bytes 100
  84.4 3.4 %copy-start.4 = (s32[1024]{0:T(1024)S(1)}, s32[1024]{0:T(1024)}, u32[]{:S(2)}) copy-start(s32[1024]{0:T(1024)} %param.19) | copy-start | bytes 12292
  84.4 3.6 %copy-start.5 = (s32[8]{0:T(128)S(1)}, s32[8]{0:T(128)}, u32[]{:S(2)}) copy-start(s32[8]{0:T(128)} %param.17) | copy-start | bytes 100
  84.4 53.8 %copy-start.2 = (f32[1664]{0:T(1024)S(1)}, f32[1664]{0:T(1024)}, u32[]{:S(2)}) copy-start(f32[1664]{0:T(1024)} %param.28) | copy-start | bytes 19972
  84.4 53.8 %copy-start.3 = (f32[1664]{0:T(1024)S(1)}, f32[1664]{0:T(1024)}, u32[]{:S(2)}) copy-start(f32[1664]{0:T(1024)} %param.27) | copy-start | bytes 19972
  84.5 118.1 %all-gather.5.cloned.1.call-start = ((), (), s32[]{:S(2)}) async-start(), calls=%async_computation.7 | async-start | bytes 7667712 | tf_op jit(solution)/shard_map/all_gather | solution.py:72
  87.6 135.6 %all-gather.3.cloned.1.call-start = ((), (), s32[]{:S(2)}) async-start(), calls=%async_computation.6 | async-start | bytes 2293760 | tf_op jit(solution)/shard_map/all_gather | solution.py:132
  137.5 0.8 copy-start.1
Sparse Core Ops, SparseCore 0:
  36.2 42.3 reduce-scatter.2
  84.6 23.6 reduce-scatter.4
Sparse Core Ops, SparseCore 1:
  87.6 114.8 all-gather.4
  204.0 19.1 all-gather.2

commit v2 on v0

v2 whole, which is shorter than its diff:
```python
import functools
import math

import jax
import jax.numpy as jnp
from jax import lax
from jax.experimental import pallas as pl
from jax.experimental.pallas import tpu as pltpu
from jax.sharding import PartitionSpec as P

HEAD_DIM = 104
TAG_PAD = 128
EPSILON = 1e-06


VMEM_BYTES = 56 * 2**20
MESH = pl.DeviceIdType.MESH


def front_kernel(
    sizes,
    places_ref,
    marks_ref,
    len_row_ref,
    len_col_ref,
    own_col_ref,
    gain2_ref,
    bias2_ref,
    up_bias_ref,
    down_bias_ref,
    gain3_ref,
    bias3_ref,
    residual_hbm,
    up_hbm,
    down_hbm,
    proj_hbm,
    merged_ref,
    everyone_ref,
    residual_ref,
    up_ref,
    down_ref,
    proj_ref,
    xq_ref,
    hidden_ref,
    acc_ref,
    core_out_ref,
    core_in_ref,
    y_out_ref,
    y_in_ref,
    share_ref,
    share_in_ref,
    out_ref,
    in_ref,
    load_sem,
    core_send,
    core_recv,
    y_send,
    y_recv,
    share_send,
    share_recv,
    req_send,
    req_recv,
    all_send,
    all_recv,
):
    senders, slots, pad = sizes
    lanes = 4
    m = lax.axis_index("mlp")
    r = lax.axis_index("req")
    core_peer = m + 1 - 2 * (m % 2)
    y_peer = (m + 2) % lanes
    own_rows = places_ref.shape[-1]
    merged = own_rows // 4
    width = residual_ref.shape[1]
    wide = out_ref.shape[1]

    loads = [
        pltpu.make_async_copy(a, b, load_sem.at[i])
        for i, (a, b) in enumerate(
            ((residual_hbm, residual_ref), (up_hbm, up_ref), (down_hbm, down_ref), (proj_hbm, proj_ref))
        )
    ]
    for load in loads:
        load.start()

    barrier = pltpu.get_barrier_semaphore()
    for k in range(1, lanes):
        pl.semaphore_signal(barrier, inc=1, device_id={"mlp": (m + k) % lanes}, device_id_type=MESH)

    def greet(k, c):
        pl.semaphore_signal(barrier, inc=1, device_id={"req": (r + k) % senders}, device_id_type=MESH)
        return c

    lax.fori_loop(1, senders, greet, 0)
    pl.semaphore_wait(barrier, lanes - 1 + senders - 1)

    def norm(values, gain, bias):
        mean_value = jnp.mean(values, axis=-1, keepdims=True)
        centred = values - mean_value
        spread = jnp.mean(centred * centred, axis=-1, keepdims=True)
        return centred * lax.rsqrt(spread + EPSILON) * gain + bias

    def core_copy(i):
        return pltpu.make_async_remote_copy(
            src_ref=core_out_ref.at[i], dst_ref=core_in_ref.at[i],
            send_sem=core_send.at[i], recv_sem=core_recv.at[i],
            device_id={"mlp": core_peer}, device_id_type=MESH,
        )

    y_copy = pltpu.make_async_remote_copy(
        src_ref=y_out_ref, dst_ref=y_in_ref, send_sem=y_send, recv_sem=y_recv,
        device_id={"mlp": y_peer}, device_id_type=MESH,
    )

    loads[0].wait()

    def quadrant_step(step, c):
        first = 1 - step // 2
        second = 1 - step % 2
        q = (1 - second) * m + second * core_peer
        q = (1 - first) * q + first * ((q + 2) % lanes)
        want = 4 * lax.broadcasted_iota(jnp.int32, (merged, own_rows), 0) + q
        for b in range(lanes):
            hits = (want == places_ref[b]).astype(jnp.float32).astype(jnp.bfloat16)
            xq_ref[b * merged : (b + 1) * merged, :] = jnp.dot(
                hits,
                residual_ref[b * own_rows : (b + 1) * own_rows, :],
                preferred_element_type=jnp.float32,
            )
        normed = norm(xq_ref[...], gain2_ref[...], bias2_ref[...]).astype(jnp.bfloat16)

        @pl.when(step == 0)
        def _():
            loads[1].wait()

        hidden_total = up_ref.shape[0]
        for j in range(0, hidden_total, 256):
            upward = lax.dot_general(
                normed, up_ref[j : j + 256, :], (((1,), (1,)), ((), ())),
                preferred_element_type=jnp.float32,
            ) + up_bias_ref[:, j : j + 256]
            hidden_ref[:, j : j + 256] = (
                0.5 * upward * (1.0 + lax.erf(upward * math.sqrt(0.5)))
            ).astype(jnp.bfloat16)

        @pl.when(step == 0)
        def _():
            loads[2].wait()

        acc_ref[...] = jnp.dot(hidden_ref[...], down_ref[...], preferred_element_type=jnp.float32)

        @pl.when(step == 0)
        def _():
            core_out_ref[0] = acc_ref[...].astype(jnp.bfloat16)
            core_copy(0).start()

        @pl.when(step == 1)
        def _():
            core_copy(0).wait_recv()
            y_out_ref[...] = (acc_ref[...] + core_in_ref[0].astype(jnp.float32)).astype(jnp.bfloat16)
            y_copy.start()

        @pl.when(step == 2)
        def _():
            core_out_ref[1] = acc_ref[...].astype(jnp.bfloat16)
            core_copy(1).start()

        return c

    lax.fori_loop(0, lanes, quadrant_step, 0)
    counts_row = len_row_ref[...] // 4
    counts_col = len_col_ref[...] // 4
    before = (
        lax.broadcasted_iota(jnp.int32, (senders, senders), 1)
        < lax.broadcasted_iota(jnp.int32, (senders, senders), 0)
    )
    starts = jnp.sum(jnp.where(before, counts_row, 0), axis=1, keepdims=True)
    index = lax.broadcasted_iota(jnp.int32, (senders, merged), 1)
    inside = (index >= starts) & (index < starts + counts_col)
    owner_of = jnp.sum(jnp.where(inside, own_col_ref[...], 0), axis=0, keepdims=True)
    begun = jnp.sum(jnp.where(inside, starts, 0), axis=0, keepdims=True)
    target = owner_of * pad + index[0:1, :] - begun
    route = (
        lax.broadcasted_iota(jnp.int32, (senders * pad, merged), 0) == target
    ).astype(jnp.float32).astype(jnp.bfloat16)
    first_hits = 4 * lax.broadcasted_iota(jnp.int32, (merged, own_rows), 0) == places_ref[m]
    row_tag = 1 + jnp.sum(jnp.where(first_hits, marks_ref[m], 0), axis=1, keepdims=True)
    tag_columns = jnp.broadcast_to(row_tag.astype(jnp.float32), (merged, wide - width))

    core_copy(1).wait_recv()
    y_copy.wait_recv()
    layer_out = (
        xq_ref[...] + (acc_ref[...] + core_in_ref[1].astype(jnp.float32) + y_in_ref[...].astype(jnp.float32))
        + down_bias_ref[...]
    ).astype(jnp.bfloat16)
    loads[3].wait()
    acc_ref[...] = jnp.dot(layer_out, proj_ref[...], preferred_element_type=jnp.float32)
    for b in range(lanes):
        share_ref[b] = acc_ref[b * merged : (b + 1) * merged, :].astype(jnp.bfloat16)
    shares = [
        pltpu.make_async_remote_copy(
            src_ref=share_ref.at[(m + k) % lanes], dst_ref=share_in_ref.at[k - 1],
            send_sem=share_send.at[k - 1], recv_sem=share_recv.at[k - 1],
            device_id={"mlp": (m + k) % lanes}, device_id_type=MESH,
        )
        for k in range(1, lanes)
    ]
    for share in shares:
        share.start()
    for share in shares:
        share.wait_recv()
    total = share_ref[m].astype(jnp.float32)
    for k in range(1, lanes):
        total = total + share_in_ref[k - 1].astype(jnp.float32)
    extended = jnp.concatenate([total, tag_columns], axis=1).astype(jnp.bfloat16)
    out_ref[...] = jnp.dot(route, extended, preferred_element_type=jnp.float32).astype(jnp.bfloat16)

    def req_copy(k):
        to = (r + k) % senders
        return pltpu.make_async_remote_copy(
            src_ref=out_ref.at[pl.ds(pl.multiple_of(to * pad, 16), pad)],
            dst_ref=in_ref.at[pl.ds(pl.multiple_of(r * pad, 16), pad)],
            send_sem=req_send.at[k - 1], recv_sem=req_recv.at[k - 1],
            device_id={"req": to}, device_id_type=MESH,
        )

    def start_req(k, c):
        req_copy(k).start()
        return c

    lax.fori_loop(1, senders, start_req, 0)
    own = pl.ds(pl.multiple_of(r * pad, 16), pad)
    in_ref[own, :] = out_ref[own, :]
    def wait_req(k, c):
        req_copy(k).wait_recv()
        return c

    lax.fori_loop(1, senders, wait_req, 0)
    arrived = in_ref[...]
    if pad != slots:
        row = lax.broadcasted_iota(jnp.int32, (senders * slots, senders * pad), 0)
        column = lax.broadcasted_iota(jnp.int32, (senders * slots, senders * pad), 1)
        pick = (row // slots * pad + row % slots == column).astype(jnp.float32).astype(jnp.bfloat16)
        arrived = jnp.dot(pick, arrived, preferred_element_type=jnp.float32).astype(jnp.bfloat16)
    received = arrived[:, :width]
    merged_ref[...] = received
    everyone_ref[m, :, width:] = arrived[:, width:]
    everyone_ref[m, :, :width] = norm(
        received.astype(jnp.float32), gain3_ref[...], bias3_ref[...]
    ).astype(jnp.bfloat16)

    def row_copy(slot, block, peer):
        return pltpu.make_async_remote_copy(
            src_ref=everyone_ref.at[block], dst_ref=everyone_ref.at[block],
            send_sem=all_send.at[slot], recv_sem=all_recv.at[slot],
            device_id={"mlp": peer}, device_id_type=MESH,
        )

    row_y = row_copy(0, m, y_peer)
    row_core = row_copy(1, m, core_peer)
    row_y.start()
    row_core.start()
    row_y.wait_recv()
    row_far = row_copy(2, y_peer, core_peer)
    row_far.start()
    row_core.wait_recv()
    row_far.wait_recv()
    for copy in (core_copy(0), core_copy(1), y_copy, *shares, row_y, row_core, row_far):
        copy.wait_send()

    def drain(k, c):
        req_copy(k).wait_send()
        return c

    lax.fori_loop(1, senders, drain, 0)


def front(places, marks, lengths, owners, residual_in, norm2_gain, norm2_bias, up_weight, up_bias,
          down_weight, down_bias, proj_weight, norm3_gain, norm3_bias):
    lanes, _, own_rows = places.shape
    senders = lengths.shape[0]
    width = residual_in.shape[1]
    merged = own_rows // 4
    slots = 2 * merged // senders
    pad = -(-slots // 16) * 16
    recv_rows = senders * slots
    wide = width + TAG_PAD
    hidden_own = up_weight.shape[0]
    bf16, f32 = jnp.bfloat16, jnp.float32
    small = [
        places, marks, lengths.reshape(1, -1), lengths.reshape(-1, 1), owners.reshape(-1, 1),
        norm2_gain.reshape(1, -1), norm2_bias.reshape(1, -1), up_bias.reshape(1, -1),
        down_bias.reshape(1, -1), norm3_gain.reshape(1, -1), norm3_bias.reshape(1, -1),
    ]
    large = [residual_in, up_weight, down_weight, proj_weight]
    dma = pltpu.SemaphoreType.DMA
    flops = 2 * own_rows * lanes * width * hidden_own * 2 + 2 * own_rows * width * width
    return pl.pallas_call(
        functools.partial(front_kernel, (senders, slots, pad)),
        out_shape=(
            jax.ShapeDtypeStruct((recv_rows, width), bf16),
            jax.ShapeDtypeStruct((lanes, recv_rows, wide), bf16),
        ),
        in_specs=[pl.BlockSpec(memory_space=pltpu.VMEM)] * len(small)
        + [pl.BlockSpec(memory_space=pl.ANY)] * len(large),
        out_specs=(pl.BlockSpec(memory_space=pltpu.VMEM),) * 2,
        scratch_shapes=[
            pltpu.VMEM(residual_in.shape, bf16),
            pltpu.VMEM(up_weight.shape, bf16),
            pltpu.VMEM(down_weight.shape, bf16),
            pltpu.VMEM(proj_weight.shape, bf16),
            pltpu.VMEM((own_rows, width), f32),
            pltpu.VMEM((own_rows, hidden_own), bf16),
            pltpu.VMEM((own_rows, width), f32),
            pltpu.VMEM((2, own_rows, width), bf16),
            pltpu.VMEM((2, own_rows, width), bf16),
            pltpu.VMEM((own_rows, width), bf16),
            pltpu.VMEM((own_rows, width), bf16),
            pltpu.VMEM((lanes, merged, width), bf16),
            pltpu.VMEM((lanes - 1, merged, width), bf16),
            pltpu.VMEM((senders * pad, wide), bf16),
            pltpu.VMEM((senders * pad, wide), bf16),
            dma((4,)),
            dma((2,)), dma((2,)), dma, dma,
            dma((lanes - 1,)), dma((lanes - 1,)),
            dma((senders - 1,)), dma((senders - 1,)),
            dma((3,)), dma((3,)),
        ],
        compiler_params=pltpu.CompilerParams(
            collective_id=0, has_side_effects=True, vmem_limit_bytes=VMEM_BYTES
        ),
        cost_estimate=pl.CostEstimate(flops=flops * 4, bytes_accessed=64 * 2**20, transcendentals=0),
        name="front",
    )(*small, *large)


def block_attention(heads_in, slot_tags):
    queries = heads_in[:, :, 0]
    key_rows = heads_in[:, :, 1]
    value_rows = heads_in[:, :, 2]
    score_scale = 1.0 / math.sqrt(heads_in.shape[-1])
    scores = (
        jnp.einsum("bqhe,bkhe->bhqk", queries, key_rows, preferred_element_type=jnp.float32)
        * score_scale
    )
    slot_total = heads_in.shape[1]
    itself = lax.broadcasted_iota(jnp.int32, (slot_total, slot_total), 0) == lax.broadcasted_iota(
        jnp.int32, (slot_total, slot_total), 1
    )
    live_slots = slot_tags >= 0
    same_request = slot_tags[:, :, None] == slot_tags[:, None, :]
    allowed = same_request & live_slots[:, None, :] | itself[None]
    weights = jnp.where(allowed[:, None], jnp.exp(scores), 0.0)
    probs = (weights / jnp.sum(weights, axis=-1, keepdims=True)).astype(jnp.bfloat16)
    mixed_out = jnp.einsum("bhqk,bkhe->bqhe", probs, value_rows, preferred_element_type=jnp.float32)
    mixed_out = jnp.where(live_slots[:, :, None, None], mixed_out, 0.0)
    return mixed_out.astype(jnp.bfloat16)


def body(
    residual_in,
    lengths,
    owners,
    merge_dest,
    segment_ids,
    norm2_gain,
    norm2_bias,
    up_weight,
    up_bias,
    down_weight,
    down_bias,
    proj_weight,
    norm3_gain,
    norm3_bias,
    next_weight,
):
    group_rows, model_width = residual_in.shape
    lane_count = lax.axis_size("mlp")
    sender_count = lax.axis_size("req")
    lane_index = lax.axis_index("mlp")
    own_rows = group_rows // lane_count
    merged_rows = own_rows // 4
    slot_count = 2 * merged_rows // sender_count
    part_width = model_width // lane_count
    own_columns = lax.dynamic_slice_in_dim(
        next_weight.transpose(1, 0, 2), lane_index * part_width, part_width, 2
    )
    piece = lax.all_gather(own_columns, "req", axis=1, tiled=True)
    received, everyone = front(
        merge_dest.reshape(lane_count, 1, own_rows),
        segment_ids.reshape(lane_count, 1, own_rows),
        lengths, owners, residual_in, norm2_gain, norm2_bias, up_weight, up_bias,
        down_weight, down_bias, proj_weight, norm3_gain, norm3_bias,
    )
    recv_rows = received.shape[0]
    everyone = everyone.reshape(lane_count * recv_rows, -1)
    tags = everyone[:, model_width].astype(jnp.int32).reshape(lane_count, recv_rows) - 1
    heads_in = jnp.einsum(
        "rd,sde->rse", everyone[:, :model_width], piece, preferred_element_type=jnp.float32
    )
    heads_in = heads_in.astype(jnp.bfloat16).reshape(lane_count, recv_rows, 3, -1, HEAD_DIM)
    mixed = block_attention(heads_in, tags).reshape(lane_count * recv_rows, part_width)
    next_mixed = lax.all_to_all(mixed, "mlp", split_axis=0, concat_axis=1, tiled=True)
    return (received, next_mixed)


def solution(mesh):
    return jax.shard_map(
        body,
        mesh=mesh,
        in_specs=(
            P("req", None),
            P(("req", "mlp")),
            P(("req", "mlp")),
            P("req"),
            P("req"),
            P(),
            P(),
            P("mlp", None),
            P("mlp"),
            P("mlp", None),
            P(),
            P("mlp", None),
            P(),
            P(),
            P("req", None, None),
        ),
        out_specs=(P(("req", "mlp"), None), P(("req", "mlp"), None)),
        check_vma=False,
    )
```

time: 414 us -> 162 us (0.39)
  waiting for transfers between devices: 289 us -> 48.3 us
  Pallas kernels: 0 us -> 69.3 us
  matrix products: 44.1 us -> 11.4 us
  local copies, waits for them, and re-layouts: 42 us -> 13.2 us
  other arithmetic: 11.3 us -> 1.28 us
  starting transfers between devices: 11.1 us -> 3.5 us
    all_gather x1, waiting for transfers between devices: 180 us -> 40.5 us  [body(): piece = lax.all_gather(own_columns, 'req', axis=1, tiled=True)]
    pallas_call x0 -> x1, Pallas kernels: none -> 69.3 us  [front(): pl.pallas_call(functools.partial(front_kernel, (senders, slots, pad)), ou...]
    psum x1 -> x0, waiting for transfers between devices: 68.8 us -> none  [body(): lax.psum(partial_sums.astype(jnp.bfloat16), 'mlp').astype(jnp.float32)]
    dot_general x4 -> x1, matrix products: 38.6 us -> 7.28 us  [body(): jnp.einsum('rd,sde->rse', everyone[:, :model_width], piece, preferred_ele...]
    all_gather x1 -> x0, local copies, waits for them, and re-layouts: 23.9 us -> none  [body(): piece = lax.all_gather(next_weight, 'req', axis=0, tiled=True)]
    all_to_all x2 -> x1, waiting for transfers between devices: 23.8 us -> 7.76 us  [body(): lax.all_to_all(mixed, 'mlp', split_axis=0, concat_axis=1, tiled=True)]
    reduce_scatter x1 -> x0, waiting for transfers between devices: 15.9 us -> none  [body(): lax.psum_scatter(jnp.dot(quarter, proj_weight, preferred_element_type=jnp...]
    all_to_all x2 -> x1, starting transfers between devices: 11 us -> 3.46 us  [body(): lax.all_to_all(mixed, 'mlp', split_axis=0, concat_axis=1, tiled=True)]
  transfers between devices with their start and end apart: 5 -> 2, of which waited for: 4 -> 2; matrix products, arithmetic and copies ran while one was open for 3% -> 3% of each run, Pallas kernels for 0% -> 43%
where the time goes in v2:
time: 162 us; the launch traced here: 161 us
  Pallas kernels  69.3 us (43%)
  waiting for transfers between devices  48.3 us (30%)
  between operations  14.2 us (9%)
  local copies, waits for them, and re-layouts  13.2 us (8%)
  matrix products  11.4 us (7%)
  starting transfers between devices  3.5 us (2%)
    pallas_call x1, Pallas kernels, front(): pl.pallas_call(functools.partial(front_kernel, (senders, slots, pad)), ou...  69.3 us
    all_gather x1, waiting for transfers between devices, body(): piece = lax.all_gather(own_columns, 'req', axis=1, tiled=True)  40.5 us
    all_to_all x1, waiting for transfers between devices, body(): lax.all_to_all(mixed, 'mlp', split_axis=0, concat_axis=1, tiled=True)  7.76 us
    dot_general x1, matrix products, body(): jnp.einsum('rd,sde->rse', everyone[:, :model_width], piece, preferred_ele...  7.28 us
    unnamed x23, local copies, waits for them, and re-layouts  4.77 us
    all_to_all x1, starting transfers between devices, body(): lax.all_to_all(mixed, 'mlp', split_axis=0, concat_axis=1, tiled=True)  3.46 us
  transfers between devices with their start and end apart: 2, of which 2 were waited for; matrix products, arithmetic and copies ran while one was open for 3% of the time, Pallas kernels for 43%

profile of v2, /device:TPU:0, one launch (start us, length us, event | category | flops | bytes accessed | tf_op | source)
XLA Modules:
  0.0 161.2 jit_solution(17395631734014131259)
XLA Ops:
  7.2 0.0 copy-start
  7.2 0.0 copy-start.3
  7.2 0.0 copy-start.4
  7.2 0.0 copy-start.5
  7.2 0.0 copy-start.6
  7.2 0.0 copy-start.7
  7.2 0.0 copy-start.9
  7.2 0.0 copy-start.8
  7.3 0.0 all-gather.2.cloned.1.call-start
  7.3 1.5 copy-done
  8.8 0.3 constant_dynamic-slice_fusion
  9.1 1.5 copy.62
  10.6 0.0 all-gather.2.cloned.1.call-update
  10.6 0.0 copy-done.3
  10.6 0.6 reshape.92.gain2_ref
  11.2 0.0 copy-done.4
  11.3 0.6 reshape.93.bias2_ref
  11.8 0.0 copy-done.5
  11.9 0.6 reshape.95.down_bias_ref
  12.4 0.0 copy-done.6
  12.5 0.6 reshape.96.gain3_ref
  13.1 0.0 copy-done.7
  13.1 0.6 reshape.97.bias3_ref
  13.7 0.0 copy-done.9
  13.7 0.7 copy.33.len_col_ref
  14.3 0.0 copy-done.8
  14.3 0.7 copy.34.own_col_ref
  15.0 69.3 %front.1 = (bf16[128,1664]{1,0:T(8,128)(2,1)}, bf16[4,128,1792]{2,1,0:T(8,128)(2,1)}) custom-call(s32[4,1,256]{2,1,0:T(1,128)} %bitcast.47, s32[4,1,256]{2,1,0:T(1,128)} %bitcast.48, s32[1,8]{1,0:T(1,128)} %bitcast.45, s32[8,1]{1,0:T(8,128)} %copy.33.len_col_ref, s32[8,1]{1,0:T(8,128)} %copy.34.own_col_ref, f32[1,1664]{1,0:T(1,128)} %reshape.92.gain2_ref, ...), custom_call_target="tpu_custom_call" | custom-call | flops 33587986432 | bytes 67108864 | tf_op jit(solution)/shard_map/front/pallas_call | solution.py:298
  84.3 1.1 add_reduce_fusion
  85.4 0.2 and_or_fusion
  85.6 40.5 %all-gather.2.cloned.1.call-done = bf16[3,1664,416]{2,0,1:T(4,128)(2,1)} async-done(((bf16[3,208,416]{2,0,1:T(4,128)(2,1)}), bf16[3,1664,416]{2,0,1:T(4,128)(2,1)}) %all-gather.2.cloned.1.call-update) | async-done | bytes 4153360 | tf_op jit(solution)/shard_map/all_gather | solution.py:388
  126.1 7.3 %fusion.2 = bf16[512,3,416]{0,2,1:T(8,128)(2,1)} fusion(bf16[3,1664,416]{2,0,1:T(4,128)(2,1)} %all-gather.2.cloned.1.call-done, bf16[512,1792]{1,0:T(8,128)(2,1)} %bitcast.43), kind=kOutput, calls=%fused_computation.3 | convolution fusion | flops 2127151104 | bytes 9797632 | tf_op jit(solution)/shard_map/rd,sde->rse/dot_general | solution.py:398
  133.4 2.6 %reshape.99 = bf16[4,128,3,4,104]{1,0,4,3,2:T(4,128)(2,1)S(1)} reshape(bf16[512,3,416]{0,2,1:T(8,128)(2,1)} %fusion.2) | data formatting | bytes 2555904 | tf_op jit(solution)/shard_map/reshape | solution.py:401
  136.1 1.2 fusion.14
  137.3 0.0 copy-start.1
  137.3 1.4 fusion.6
  138.6 0.0 copy-done.1
  138.6 0.0 copy-start.2
  138.6 2.8 %fusion.7 = bf16[4,4,104,128]{3,2,1,0:T(8,128)(2,1)} fusion(f32[4,4,128,128]{2,3,1,0:T(8,128)} %fusion.6, bf16[4,128,1,4,104]{1,0,4,3,2:T(4,128)(2,1)S(1)} %copy-done.1, pred[4,128]{1,0:T(4,128)(4,1)S(1)} %broadcast_compare_fusion), kind=kOutput, calls=%fused_computation.8 | convolution fusion | flops 55478400 | bytes 1901056 | tf_op jit(solution)/shard_map/bhqk,bkhe->bqhe/dot_general | solution.py:355
  141.4 3.5 %all-to-all-start = ((bf16[4,128,416]{1,2,0:T(8,128)(2,1)}), bf16[4,128,416]{1,2,0:T(8,128)(2,1)S(1)}, u32[]{:S(2)}, u32[]{:S(2)}) async-start(bf16[4,128,416]{1,2,0:T(8,128)(2,1)} %bitcast.13), calls=%async_computation | async-start | bytes 851968 | tf_op jit(solution)/shard_map/all_to_all | solution.py:403
  144.9 7.8 %all-to-all-done = bf16[4,128,416]{1,2,0:T(8,128)(2,1)S(1)} async-done(((bf16[4,128,416]{1,2,0:T(8,128)(2,1)}), bf16[4,128,416]{1,2,0:T(8,128)(2,1)S(1)}, u32[]{:S(2)}, u32[]{:S(2)}) %all-to-all-start) | async-done | bytes 426016 | tf_op jit(solution)/shard_map/all_to_all | solution.py:403
  152.6 1.0 copy.41
  153.6 0.0 copy-done.2
  153.6 0.8 copy.64
  (2 shorter events, 0.0 us)
Async XLA Ops:
  7.2 1.6 copy-start
  7.2 3.5 %copy-start.3 = (f32[1664]{0:T(1024)S(1)}, f32[1664]{0:T(1024)}, u32[]{:S(2)}) copy-start(f32[1664]{0:T(1024)} %param.20) | copy-start | bytes 19972
  7.2 4.1 %copy-start.4 = (f32[1664]{0:T(1024)S(1)}, f32[1664]{0:T(1024)}, u32[]{:S(2)}) copy-start(f32[1664]{0:T(1024)} %param.21) | copy-start | bytes 19972
  7.2 4.7 %copy-start.5 = (f32[1664]{0:T(1024)S(1)}, f32[1664]{0:T(1024)}, u32[]{:S(2)}) copy-start(f32[1664]{0:T(1024)} %param.25) | copy-start | bytes 19972
  7.2 5.2 %copy-start.6 = (f32[1664]{0:T(1024)S(1)}, f32[1664]{0:T(1024)}, u32[]{:S(2)}) copy-start(f32[1664]{0:T(1024)} %param.27) | copy-start | bytes 19972
  7.2 5.8 %copy-start.7 = (f32[1664]{0:T(1024)S(1)}, f32[1664]{0:T(1024)}, u32[]{:S(2)}) copy-start(f32[1664]{0:T(1024)} %param.28) | copy-start | bytes 19972
  7.2 6.4 %copy-start.9 = (s32[8]{0:T(128)S(1)}, s32[8]{0:T(128)}, u32[]{:S(2)}) copy-start(s32[8]{0:T(128)} %param.16) | copy-start | bytes 100
  7.2 7.1 %copy-start.8 = (s32[8]{0:T(128)S(1)}, s32[8]{0:T(128)}, u32[]{:S(2)}) copy-start(s32[8]{0:T(128)} %param.17) | copy-start | bytes 100
  7.3 118.9 %all-gather.2.cloned.1.call-start = ((), (), s32[]{:S(2)}) async-start(), calls=%async_computation.1 | async-start | bytes 7667712 | tf_op jit(solution)/shard_map/all_gather | solution.py:388
  137.3 1.4 copy-start.1
  138.6 15.0 %copy-start.2 = (bf16[128,1664]{1,0:T(8,128)(2,1)S(1)}, bf16[128,1664]{1,0:T(8,128)(2,1)}, u32[]{:S(2)}) copy-start(bf16[128,1664]{1,0:T(8,128)(2,1)} %get-tuple-element.15) | copy-start | bytes 1277956
  141.4 11.2 %all-to-all-start = ((bf16[4,128,416]{1,2,0:T(8,128)(2,1)}), bf16[4,128,416]{1,2,0:T(8,128)(2,1)S(1)}, u32[]{:S(2)}, u32[]{:S(2)}) async-start(bf16[4,128,416]{1,2,0:T(8,128)(2,1)} %bitcast.13), calls=%async_computation | async-start | bytes 851968 | tf_op jit(solution)/shard_map/all_to_all | solution.py:403
Sparse Core Ops, SparseCore 0:
  10.8 115.3 all-gather.1

commit v3 on v2

--- a/solution.py
+++ b/solution.py
@@ -19,6 +19,7 @@
 
 def front_kernel(
     sizes,
+    gather,
     places_ref,
     marks_ref,
     len_row_ref,
@@ -34,8 +35,12 @@
     up_hbm,
     down_hbm,
     proj_hbm,
+    next_hbm,
     merged_ref,
+    mixed_ref,
     everyone_ref,
+    next_ref,
+    mix_ref,
     residual_ref,
     up_ref,
     down_ref,
@@ -62,6 +67,10 @@
     req_recv,
     all_send,
     all_recv,
+    next_send,
+    next_recv,
+    mix_send,
+    mix_recv,
 ):
     senders, slots, pad = sizes
     lanes = 4
@@ -73,11 +82,39 @@
     merged = own_rows // 4
     width = residual_ref.shape[1]
     wide = out_ref.shape[1]
+    shard_rows = next_hbm.shape[0]
+    heights = senders // 2
+    x_peer = r + 1 - 2 * (r % 2)
+
+    def shard(index):
+        return pl.ds(pl.multiple_of(index * shard_rows, 16), shard_rows)
+
+    def next_copy(slot, index, peer):
+        return pltpu.make_async_remote_copy(
+            src_ref=next_ref.at[shard(index)], dst_ref=next_ref.at[shard(index)],
+            send_sem=next_send.at[slot], recv_sem=next_recv.at[slot],
+            device_id={"req": peer}, device_id_type=MESH,
+        )
+
+    def z_copy(k):
+        return next_copy(k, r, (r + 2 * k) % senders)
+
+    def forward(k):
+        return next_copy(heights - 1 + k, (r + senders - 2 * k) % senders, x_peer)
+
+    def pass_on(k):
+        if gather:
+            z_copy(k).wait_recv()
+            forward(k).start()
+
 
     loads = [
         pltpu.make_async_copy(a, b, load_sem.at[i])
         for i, (a, b) in enumerate(
-            ((residual_hbm, residual_ref), (up_hbm, up_ref), (down_hbm, down_ref), (proj_hbm, proj_ref))
+            (
+                (residual_hbm, residual_ref), (up_hbm, up_ref), (down_hbm, down_ref), (proj_hbm, proj_ref),
+                (next_hbm, next_ref.at[shard(r)] if gather else next_ref),
+            )
         )
     ]
     for load in loads:
@@ -111,6 +148,12 @@
         src_ref=y_out_ref, dst_ref=y_in_ref, send_sem=y_send, recv_sem=y_recv,
         device_id={"mlp": y_peer}, device_id_type=MESH,
     )
+
+    if gather:
+        loads[4].wait()
+        next_copy(0, r, x_peer).start()
+        for k in range(1, heights):
+            z_copy(k).start()
 
     loads[0].wait()
 
@@ -207,6 +250,8 @@
     ]
     for share in shares:
         share.start()
+    for k in range(1, heights, 2):
+        pass_on(k)
     for share in shares:
         share.wait_recv()
     total = share_ref[m].astype(jnp.float32)
@@ -229,6 +274,8 @@
         return c
 
     lax.fori_loop(1, senders, start_req, 0)
+    for k in range(2, heights, 2):
+        pass_on(k)
     own = pl.ds(pl.multiple_of(r * pad, 16), pad)
     in_ref[own, :] = out_ref[own, :]
     def wait_req(k, c):
@@ -260,11 +307,81 @@
     row_core = row_copy(1, m, core_peer)
     row_y.start()
     row_core.start()
-    row_y.wait_recv()
+    if gather:
+        for k in range(heights):
+            if k:
+                forward(k).wait_recv()
+            else:
+                next_copy(0, r, x_peer).wait_recv()
+    else:
+        loads[4].wait()
+    part = next_ref.shape[1] // 3
+    score_scale = 1.0 / math.sqrt(HEAD_DIM)
+    recv_rows = senders * slots
+    itself = lax.broadcasted_iota(jnp.int32, (recv_rows, recv_rows), 0) == lax.broadcasted_iota(
+        jnp.int32, (recv_rows, recv_rows), 1
+    )
     row_far = row_copy(2, y_peer, core_peer)
-    row_far.start()
-    row_core.wait_recv()
-    row_far.wait_recv()
+
+    def block_of(step):
+        first = step // 2
+        second = step % 2
+        block = (1 - second) * m + second * core_peer
+        return (1 - first) * block + first * ((block + 2) % lanes)
+
+    def mix_copy(step):
+        return pltpu.make_async_remote_copy(
+            src_ref=mix_ref.at[block_of(step)], dst_ref=mixed_ref.at[m],
+            send_sem=mix_send.at[step - 1], recv_sem=mix_recv.at[step - 1],
+            device_id={"mlp": block_of(step)}, device_id_type=MESH,
+        )
+
+    def attend(step, c):
+        @pl.when(step == 1)
+        def _():
+            row_core.wait_recv()
+
+        @pl.when(step == 2)
+        def _():
+            row_y.wait_recv()
+            row_far.start()
+
+        @pl.when(step == 3)
+        def _():
+            row_far.wait_recv()
+
+        block = block_of(step)
+        rows = everyone_ref[block]
+        heads = jnp.dot(rows[:, :width], next_ref[...], preferred_element_type=jnp.float32)
+        tags = rows[:, width : width + recv_rows].astype(jnp.float32)
+        key_tags = tags.T
+        allowed = ((tags == key_tags) & (key_tags > 0.5)) | itself
+        live = tags[:, :1] > 0.5
+        outs = []
+        for h in range(part // HEAD_DIM):
+            at = h * HEAD_DIM
+            query, key, value = (
+                heads[:, i * part + at : i * part + at + HEAD_DIM].astype(jnp.bfloat16) for i in range(3)
+            )
+            scores = lax.dot_general(
+                query, key, (((1,), (1,)), ((), ())), preferred_element_type=jnp.float32
+            ) * score_scale
+            weights = jnp.where(allowed, jnp.exp(scores), 0.0)
+            probs = (weights / jnp.sum(weights, axis=-1, keepdims=True)).astype(jnp.bfloat16)
+            mixed = jnp.dot(probs, value, preferred_element_type=jnp.float32)
+            outs.append(jnp.where(live, mixed, 0.0))
+        mix_ref[block] = jnp.concatenate(outs, axis=1).astype(jnp.bfloat16)
+
+        @pl.when(step > 0)
+        def _():
+            mix_copy(step).start()
+
+        return c
+
+    lax.fori_loop(0, lanes, attend, 0)
+    mixed_ref[m] = mix_ref[m]
+    for step in range(1, lanes):
+        mix_copy(step).wait()
     for copy in (core_copy(0), core_copy(1), y_copy, *shares, row_y, row_core, row_far):
         copy.wait_send()
 
@@ -273,10 +390,15 @@
         return c
 
     lax.fori_loop(1, senders, drain, 0)
+    if gather:
+        next_copy(0, r, x_peer).wait_send()
+        for k in range(1, heights):
+            z_copy(k).wait_send()
+            forward(k).wait_send()
 
 
 def front(places, marks, lengths, owners, residual_in, norm2_gain, norm2_bias, up_weight, up_bias,
-          down_weight, down_bias, proj_weight, norm3_gain, norm3_bias):
+          down_weight, down_bias, proj_weight, norm3_gain, norm3_bias, next_part, gather):
     lanes, _, own_rows = places.shape
     senders = lengths.shape[0]
     width = residual_in.shape[1]
@@ -292,19 +414,22 @@
         norm2_gain.reshape(1, -1), norm2_bias.reshape(1, -1), up_bias.reshape(1, -1),
         down_bias.reshape(1, -1), norm3_gain.reshape(1, -1), norm3_bias.reshape(1, -1),
     ]
-    large = [residual_in, up_weight, down_weight, proj_weight]
+    large = [residual_in, up_weight, down_weight, proj_weight, next_part]
     dma = pltpu.SemaphoreType.DMA
     flops = 2 * own_rows * lanes * width * hidden_own * 2 + 2 * own_rows * width * width
     return pl.pallas_call(
-        functools.partial(front_kernel, (senders, slots, pad)),
+        functools.partial(front_kernel, (senders, slots, pad), gather),
         out_shape=(
             jax.ShapeDtypeStruct((recv_rows, width), bf16),
-            jax.ShapeDtypeStruct((lanes, recv_rows, wide), bf16),
+            jax.ShapeDtypeStruct((lanes, recv_rows, next_part.shape[1] // 3), bf16),
         ),
         in_specs=[pl.BlockSpec(memory_space=pltpu.VMEM)] * len(small)
         + [pl.BlockSpec(memory_space=pl.ANY)] * len(large),
         out_specs=(pl.BlockSpec(memory_space=pltpu.VMEM),) * 2,
         scratch_shapes=[
+            pltpu.VMEM((lanes, recv_rows, wide), bf16),
+            pltpu.VMEM((width, next_part.shape[1]), bf16),
+            pltpu.VMEM((lanes, recv_rows, next_part.shape[1] // 3), bf16),
             pltpu.VMEM(residual_in.shape, bf16),
             pltpu.VMEM(up_weight.shape, bf16),
             pltpu.VMEM(down_weight.shape, bf16),
@@ -320,11 +445,13 @@
             pltpu.VMEM((lanes - 1, merged, width), bf16),
             pltpu.VMEM((senders * pad, wide), bf16),
             pltpu.VMEM((senders * pad, wide), bf16),
-            dma((4,)),
+            dma((5,)),
             dma((2,)), dma((2,)), dma, dma,
             dma((lanes - 1,)), dma((lanes - 1,)),
             dma((senders - 1,)), dma((senders - 1,)),
             dma((3,)), dma((3,)),
+            dma((senders - 1,)), dma((senders - 1,)),
+            dma((lanes - 1,)), dma((lanes - 1,)),
         ],
         compiler_params=pltpu.CompilerParams(
             collective_id=0, has_side_effects=True, vmem_limit_bytes=VMEM_BYTES
@@ -332,29 +459,6 @@
         cost_estimate=pl.CostEstimate(flops=flops * 4, bytes_accessed=64 * 2**20, transcendentals=0),
         name="front",
     )(*small, *large)
-
-
-def block_attention(heads_in, slot_tags):
-    queries = heads_in[:, :, 0]
-    key_rows = heads_in[:, :, 1]
-    value_rows = heads_in[:, :, 2]
-    score_scale = 1.0 / math.sqrt(heads_in.shape[-1])
-    scores = (
-        jnp.einsum("bqhe,bkhe->bhqk", queries, key_rows, preferred_element_type=jnp.float32)
-        * score_scale
-    )
-    slot_total = heads_in.shape[1]
-    itself = lax.broadcasted_iota(jnp.int32, (slot_total, slot_total), 0) == lax.broadcasted_iota(
-        jnp.int32, (slot_total, slot_total), 1
-    )
-    live_slots = slot_tags >= 0
-    same_request = slot_tags[:, :, None] == slot_tags[:, None, :]
-    allowed = same_request & live_slots[:, None, :] | itself[None]
-    weights = jnp.where(allowed[:, None], jnp.exp(scores), 0.0)
-    probs = (weights / jnp.sum(weights, axis=-1, keepdims=True)).astype(jnp.bfloat16)
-    mixed_out = jnp.einsum("bhqk,bkhe->bqhe", probs, value_rows, preferred_element_type=jnp.float32)
-    mixed_out = jnp.where(live_slots[:, :, None, None], mixed_out, 0.0)
-    return mixed_out.astype(jnp.bfloat16)
 
 
 def body(
@@ -376,31 +480,22 @@
 ):
     group_rows, model_width = residual_in.shape
     lane_count = lax.axis_size("mlp")
-    sender_count = lax.axis_size("req")
     lane_index = lax.axis_index("mlp")
     own_rows = group_rows // lane_count
-    merged_rows = own_rows // 4
-    slot_count = 2 * merged_rows // sender_count
     part_width = model_width // lane_count
     own_columns = lax.dynamic_slice_in_dim(
-        next_weight.transpose(1, 0, 2), lane_index * part_width, part_width, 2
-    )
-    piece = lax.all_gather(own_columns, "req", axis=1, tiled=True)
-    received, everyone = front(
+        next_weight, lane_index * part_width, part_width, 2
+    ).reshape(next_weight.shape[0], -1)
+    gather = next_weight.shape[0] % 16 == 0
+    if not gather:
+        own_columns = lax.all_gather(own_columns, "req", axis=0, tiled=True)
+    received, mixed = front(
         merge_dest.reshape(lane_count, 1, own_rows),
         segment_ids.reshape(lane_count, 1, own_rows),
         lengths, owners, residual_in, norm2_gain, norm2_bias, up_weight, up_bias,
-        down_weight, down_bias, proj_weight, norm3_gain, norm3_bias,
+        down_weight, down_bias, proj_weight, norm3_gain, norm3_bias, own_columns, gather,
     )
-    recv_rows = received.shape[0]
-    everyone = everyone.reshape(lane_count * recv_rows, -1)
-    tags = everyone[:, model_width].astype(jnp.int32).reshape(lane_count, recv_rows) - 1
-    heads_in = jnp.einsum(
-        "rd,sde->rse", everyone[:, :model_width], piece, preferred_element_type=jnp.float32
-    )
-    heads_in = heads_in.astype(jnp.bfloat16).reshape(lane_count, recv_rows, 3, -1, HEAD_DIM)
-    mixed = block_attention(heads_in, tags).reshape(lane_count * recv_rows, part_width)
-    next_mixed = lax.all_to_all(mixed, "mlp", split_axis=0, concat_axis=1, tiled=True)
+    next_mixed = mixed.transpose(1, 0, 2).reshape(received.shape)
     return (received, next_mixed)
 
 

time: 162 us -> 117 us (0.72)
  the two profiles are of different devices: /device:TPU:0 before, /device:TPU:9 now
where the time goes in v3:
time: 117 us; the launch traced here: 116 us
  Pallas kernels  101 us (86%)
  local copies, waits for them, and re-layouts  14.9 us (13%)
    pallas_call x1, Pallas kernels, front(): pl.pallas_call(functools.partial(front_kernel, (senders, slots, pad), gat...  101 us
    unnamed x4, local copies, waits for them, and re-layouts  2.79 us

profile of v3, /device:TPU:9, one launch (start us, length us, event | category | flops | bytes accessed | tf_op | source)
XLA Modules:
  0.0 116.2 jit_solution(14752381938189566864)
XLA Ops:
  0.6 0.0 copy-start
  0.6 1.5 %copy.22.own_col_ref = s32[8,1]{1,0:T(8,128)} copy(s32[8,1]{0,1:T(1,128)} %bitcast.12) | data formatting | bytes 64 | tf_op jit(solution)/shard_map/reshape | solution.py:413
  2.1 1.3 %copy.21.len_col_ref = s32[8,1]{1,0:T(8,128)} copy(s32[8,1]{0,1:T(1,128)} %bitcast.13) | data formatting | bytes 64 | tf_op jit(solution)/shard_map/reshape | solution.py:413
  3.4 1.3 %reshape.48.gain2_ref = f32[1,1664]{1,0:T(1,128)} reshape(f32[1664]{0:T(1024)} %param.20) | data formatting | bytes 13312 | tf_op jit(solution)/shard_map/reshape | solution.py:414
  4.7 1.3 %reshape.49.bias2_ref = f32[1,1664]{1,0:T(1,128)} reshape(f32[1664]{0:T(1024)} %param.21) | data formatting | bytes 13312 | tf_op jit(solution)/shard_map/reshape | solution.py:414
  6.0 1.3 %reshape.51.down_bias_ref = f32[1,1664]{1,0:T(1,128)} reshape(f32[1664]{0:T(1024)} %param.25) | data formatting | bytes 13312 | tf_op jit(solution)/shard_map/reshape | solution.py:415
  7.3 1.3 %reshape.52.gain3_ref = f32[1,1664]{1,0:T(1,128)} reshape(f32[1664]{0:T(1024)} %param.27) | data formatting | bytes 13312 | tf_op jit(solution)/shard_map/reshape | solution.py:415
  8.6 1.3 %reshape.53.bias3_ref = f32[1,1664]{1,0:T(1,128)} reshape(f32[1664]{0:T(1024)} %param.28) | data formatting | bytes 13312 | tf_op jit(solution)/shard_map/reshape | solution.py:415
  9.9 0.0 copy-done
  9.9 0.3 constant_dynamic-slice_fusion
  10.2 0.3 copy.20
  10.5 1.0 copy.23.next_hbm
  11.5 100.6 %front.1 = (bf16[128,1664]{1,0:T(8,128)(2,1)}, bf16[4,128,416]{2,1,0:T(8,128)(2,1)}) custom-call(s32[4,1,256]{2,1,0:T(1,128)} %bitcast.15, s32[4,1,256]{2,1,0:T(1,128)} %bitcast.16, s32[1,8]{1,0:T(1,128)} %bitcast.14, s32[8,1]{1,0:T(8,128)} %copy.21.len_col_ref, s32[8,1]{1,0:T(8,128)} %copy.22.own_col_ref, f32[1,1664]{1,0:T(1,128)} %reshape.48.gain2_ref, ...), custom_call_target="tpu_custom_call" | custom-call | flops 33587986432 | bytes 67108864 | tf_op jit(solution)/shard_map/front/pallas_call | solution.py:420
  112.2 1.3 %copy.24 = bf16[128,4,416]{0,2,1:T(8,128)(2,1)S(1)} copy(bf16[128,4,416]{2,0,1:T(8,128)(2,1)} %bitcast.11) | data formatting | bytes 851968 | tf_op jit(solution)/shard_map/transpose | solution.py:498
  113.5 1.0 copy.25
  114.5 1.8 %copy.27 = bf16[128,1664]{1,0:T(8,128)(2,1)} copy(bf16[128,1664]{1,0:T(8,128)(2,1)} %get-tuple-element.10) | data formatting | bytes 851968
Async XLA Ops:
  0.6 9.3 %copy-start = (bf16[208,3,1664]{2,0,1:T(8,128)(2,1)S(1)}, bf16[208,3,1664]{2,0,1:T(8,128)(2,1)}, u32[]{:S(2)}) copy-start(bf16[208,3,1664]{2,0,1:T(8,128)(2,1)} %param.29) | copy-start | bytes 6230020

commit v4 on v3

--- a/solution.py
+++ b/solution.py
@@ -22,21 +22,17 @@
     gather,
     places_ref,
     marks_ref,
-    len_row_ref,
-    len_col_ref,
-    own_col_ref,
-    gain2_ref,
-    bias2_ref,
+    len_ref,
+    owner_ref,
     up_bias_ref,
-    down_bias_ref,
-    gain3_ref,
-    bias3_ref,
+    params_ref,
     residual_hbm,
     up_hbm,
     down_hbm,
     proj_hbm,
     next_hbm,
     merged_ref,
+    next_mixed_ref,
     mixed_ref,
     everyone_ref,
     next_ref,
@@ -53,6 +49,7 @@
     y_out_ref,
     y_in_ref,
     share_ref,
+    share_out_ref,
     share_in_ref,
     out_ref,
     in_ref,
@@ -152,12 +149,27 @@
     if gather:
         loads[4].wait()
         next_copy(0, r, x_peer).start()
-        for k in range(1, heights):
+        for k in range(1, heights, 2):
             z_copy(k).start()
 
     loads[0].wait()
 
     def quadrant_step(step, c):
+        if gather:
+            @pl.when(step == 1)
+            def _():
+                for k in range(2, heights, 2):
+                    z_copy(k).start()
+
+            @pl.when(step == 2)
+            def _():
+                pass_on(1)
+
+            @pl.when(step == 3)
+            def _():
+                for k in range(3, heights, 2):
+                    pass_on(k)
+
         first = 1 - step // 2
         second = 1 - step % 2
         q = (1 - second) * m + second * core_peer
@@ -170,7 +182,7 @@
                 residual_ref[b * own_rows : (b + 1) * own_rows, :],
                 preferred_element_type=jnp.float32,
             )
-        normed = norm(xq_ref[...], gain2_ref[...], bias2_ref[...]).astype(jnp.bfloat16)
+        normed = norm(xq_ref[...], params_ref[0:1, :], params_ref[1:2, :]).astype(jnp.bfloat16)
 
         @pl.when(step == 0)
         def _():
@@ -211,16 +223,20 @@
         return c
 
     lax.fori_loop(0, lanes, quadrant_step, 0)
-    counts_row = len_row_ref[...] // 4
-    counts_col = len_col_ref[...] // 4
-    before = (
-        lax.broadcasted_iota(jnp.int32, (senders, senders), 1)
-        < lax.broadcasted_iota(jnp.int32, (senders, senders), 0)
+    counts_row = len_ref[...] // 4
+    down_index = lax.broadcasted_iota(jnp.int32, (senders, senders), 0)
+    across_index = lax.broadcasted_iota(jnp.int32, (senders, senders), 1)
+    counts_col = jnp.sum(
+        jnp.where(across_index == down_index, counts_row, 0), axis=1, keepdims=True
     )
+    owners_col = jnp.sum(
+        jnp.where(across_index == down_index, owner_ref[...], 0), axis=1, keepdims=True
+    )
+    before = across_index < down_index
     starts = jnp.sum(jnp.where(before, counts_row, 0), axis=1, keepdims=True)
     index = lax.broadcasted_iota(jnp.int32, (senders, merged), 1)
     inside = (index >= starts) & (index < starts + counts_col)
-    owner_of = jnp.sum(jnp.where(inside, own_col_ref[...], 0), axis=0, keepdims=True)
+    owner_of = jnp.sum(jnp.where(inside, owners_col, 0), axis=0, keepdims=True)
     begun = jnp.sum(jnp.where(inside, starts, 0), axis=0, keepdims=True)
     target = owner_of * pad + index[0:1, :] - begun
     route = (
@@ -234,29 +250,40 @@
     y_copy.wait_recv()
     layer_out = (
         xq_ref[...] + (acc_ref[...] + core_in_ref[1].astype(jnp.float32) + y_in_ref[...].astype(jnp.float32))
-        + down_bias_ref[...]
+        + params_ref[2:3, :]
     ).astype(jnp.bfloat16)
     loads[3].wait()
     acc_ref[...] = jnp.dot(layer_out, proj_ref[...], preferred_element_type=jnp.float32)
     for b in range(lanes):
         share_ref[b] = acc_ref[b * merged : (b + 1) * merged, :].astype(jnp.bfloat16)
+    far = lanes - 1 - m
+
+    def share_copy(slot, source, peer):
+        return pltpu.make_async_remote_copy(
+            src_ref=source, dst_ref=share_in_ref.at[slot],
+            send_sem=share_send.at[slot], recv_sem=share_recv.at[slot],
+            device_id={"mlp": peer}, device_id_type=MESH,
+        )
+
+    share_y = share_copy(2, share_out_ref, y_peer)
     shares = [
-        pltpu.make_async_remote_copy(
-            src_ref=share_ref.at[(m + k) % lanes], dst_ref=share_in_ref.at[k - 1],
-            send_sem=share_send.at[k - 1], recv_sem=share_recv.at[k - 1],
-            device_id={"mlp": (m + k) % lanes}, device_id_type=MESH,
-        )
-        for k in range(1, lanes)
+        share_copy(0, share_ref.at[far], core_peer),
+        share_copy(1, share_ref.at[core_peer], core_peer),
+        share_y,
     ]
-    for share in shares:
-        share.start()
-    for k in range(1, heights, 2):
+    shares[0].start()
+    shares[1].start()
+    shares[0].wait_recv()
+    share_out_ref[...] = (
+        share_ref[y_peer].astype(jnp.float32) + share_in_ref[0].astype(jnp.float32)
+    ).astype(jnp.bfloat16)
+    share_y.start()
+    for k in range(2, heights, 2):
         pass_on(k)
-    for share in shares:
-        share.wait_recv()
-    total = share_ref[m].astype(jnp.float32)
-    for k in range(1, lanes):
-        total = total + share_in_ref[k - 1].astype(jnp.float32)
+    shares[1].wait_recv()
+    total = share_ref[m].astype(jnp.float32) + share_in_ref[1].astype(jnp.float32)
+    share_y.wait_recv()
+    total = total + share_in_ref[2].astype(jnp.float32)
     extended = jnp.concatenate([total, tag_columns], axis=1).astype(jnp.bfloat16)
     out_ref[...] = jnp.dot(route, extended, preferred_element_type=jnp.float32).astype(jnp.bfloat16)
 
@@ -274,8 +301,6 @@
         return c
 
     lax.fori_loop(1, senders, start_req, 0)
-    for k in range(2, heights, 2):
-        pass_on(k)
     own = pl.ds(pl.multiple_of(r * pad, 16), pad)
     in_ref[own, :] = out_ref[own, :]
     def wait_req(k, c):
@@ -293,7 +318,7 @@
     merged_ref[...] = received
     everyone_ref[m, :, width:] = arrived[:, width:]
     everyone_ref[m, :, :width] = norm(
-        received.astype(jnp.float32), gain3_ref[...], bias3_ref[...]
+        received.astype(jnp.float32), params_ref[3:4, :], params_ref[4:5, :]
     ).astype(jnp.bfloat16)
 
     def row_copy(slot, block, peer):
@@ -382,6 +407,9 @@
     mixed_ref[m] = mix_ref[m]
     for step in range(1, lanes):
         mix_copy(step).wait()
+    next_mixed_ref[...] = jnp.concatenate(
+        [mixed_ref[b].astype(jnp.float32) for b in range(lanes)], axis=1
+    ).astype(jnp.bfloat16)
     for copy in (core_copy(0), core_copy(1), y_copy, *shares, row_y, row_core, row_far):
         copy.wait_send()
 
@@ -410,9 +438,8 @@
     hidden_own = up_weight.shape[0]
     bf16, f32 = jnp.bfloat16, jnp.float32
     small = [
-        places, marks, lengths.reshape(1, -1), lengths.reshape(-1, 1), owners.reshape(-1, 1),
-        norm2_gain.reshape(1, -1), norm2_bias.reshape(1, -1), up_bias.reshape(1, -1),
-        down_bias.reshape(1, -1), norm3_gain.reshape(1, -1), norm3_bias.reshape(1, -1),
+        places, marks, lengths.reshape(1, -1), owners.reshape(1, -1), up_bias.reshape(1, -1),
+        jnp.stack([norm2_gain, norm2_bias, down_bias, norm3_gain, norm3_bias]),
     ]
     large = [residual_in, up_weight, down_weight, proj_weight, next_part]
     dma = pltpu.SemaphoreType.DMA
@@ -421,12 +448,13 @@
         functools.partial(front_kernel, (senders, slots, pad), gather),
         out_shape=(
             jax.ShapeDtypeStruct((recv_rows, width), bf16),
-            jax.ShapeDtypeStruct((lanes, recv_rows, next_part.shape[1] // 3), bf16),
+            jax.ShapeDtypeStruct((recv_rows, width), bf16),
         ),
         in_specs=[pl.BlockSpec(memory_space=pltpu.VMEM)] * len(small)
         + [pl.BlockSpec(memory_space=pl.ANY)] * len(large),
         out_specs=(pl.BlockSpec(memory_space=pltpu.VMEM),) * 2,
         scratch_shapes=[
+            pltpu.VMEM((lanes, recv_rows, next_part.shape[1] // 3), bf16),
             pltpu.VMEM((lanes, recv_rows, wide), bf16),
             pltpu.VMEM((width, next_part.shape[1]), bf16),
             pltpu.VMEM((lanes, recv_rows, next_part.shape[1] // 3), bf16),
@@ -442,6 +470,7 @@
             pltpu.VMEM((own_rows, width), bf16),
             pltpu.VMEM((own_rows, width), bf16),
             pltpu.VMEM((lanes, merged, width), bf16),
+            pltpu.VMEM((merged, width), bf16),
             pltpu.VMEM((lanes - 1, merged, width), bf16),
             pltpu.VMEM((senders * pad, wide), bf16),
             pltpu.VMEM((senders * pad, wide), bf16),
@@ -489,14 +518,12 @@
     gather = next_weight.shape[0] % 16 == 0
     if not gather:
         own_columns = lax.all_gather(own_columns, "req", axis=0, tiled=True)
-    received, mixed = front(
+    return front(
         merge_dest.reshape(lane_count, 1, own_rows),
         segment_ids.reshape(lane_count, 1, own_rows),
         lengths, owners, residual_in, norm2_gain, norm2_bias, up_weight, up_bias,
         down_weight, down_bias, proj_weight, norm3_gain, norm3_bias, own_columns, gather,
     )
-    next_mixed = mixed.transpose(1, 0, 2).reshape(received.shape)
-    return (received, next_mixed)
 
 
 def solution(mesh):

time: 117 us -> 114 us (0.974)
  the two profiles are of different devices: /device:TPU:9 before, /device:TPU:19 now
where the time goes in v4:
time: 114 us
  Pallas kernels  104 us (91%)
  local copies, waits for them, and re-layouts  9.52 us (8%)
    pallas_call x1, Pallas kernels, front(): pl.pallas_call(functools.partial(front_kernel, (senders, slots, pad), gat...  104 us
    another operation x6, local copies, waits for them, and re-layouts, front(): jnp.stack([norm2_gain, norm2_bias, down_bias, norm3_gain, norm3_bias])  4.33 us
    unnamed x4, local copies, waits for them, and re-layouts  3.6 us

profile of v4, /device:TPU:19, one launch (start us, length us, event | category | flops | bytes accessed | tf_op | source)
XLA Modules:
  0.0 114.0 jit_solution(15737006426029937103)
XLA Ops:
  0.6 0.0 copy-start
  0.6 0.8 stack.18
  1.5 0.7 stack.19
  2.2 0.7 stack.20
  2.9 0.7 stack.21
  3.6 0.7 stack.22
  4.3 0.7 stack.23.params_ref
  5.0 0.0 copy-done
  5.0 0.3 constant_dynamic-slice_fusion
  5.3 0.3 copy.18
  5.6 1.0 copy.19.next_hbm
  6.6 103.8 %front.1 = (bf16[128,1664]{1,0:T(8,128)(2,1)}, bf16[128,1664]{1,0:T(8,128)(2,1)}) custom-call(s32[4,1,256]{2,1,0:T(1,128)} %bitcast.7, s32[4,1,256]{2,1,0:T(1,128)} %bitcast.8, s32[1,8]{1,0:T(1,128)} %bitcast.10, s32[1,8]{1,0:T(1,128)} %bitcast.11, f32[1,1024]{1,0:T(1,128)} %bitcast.9, f32[5,1664]{1,0:T(8,128)} %stack.23.params_ref, ...), custom_call_target="tpu_custom_call" | custom-call | flops 33587986432 | bytes 67108864 | tf_op jit(solution)/shard_map/front/pallas_call | solution.py:447
  110.4 1.8 %copy.22 = bf16[128,1664]{1,0:T(8,128)(2,1)} copy(bf16[128,1664]{1,0:T(8,128)(2,1)} %get-tuple-element.4) | data formatting | bytes 851968
  112.2 1.8 %copy.23 = bf16[128,1664]{1,0:T(8,128)(2,1)} copy(bf16[128,1664]{1,0:T(8,128)(2,1)} %get-tuple-element.5) | data formatting | bytes 851968
Async XLA Ops:
  0.6 4.4 %copy-start = (bf16[208,3,1664]{2,0,1:T(8,128)(2,1)S(1)}, bf16[208,3,1664]{2,0,1:T(8,128)(2,1)}, u32[]{:S(2)}) copy-start(bf16[208,3,1664]{2,0,1:T(8,128)(2,1)} %param.29) | copy-start | bytes 6230020

commit v5 on v4

--- a/solution.py
+++ b/solution.py
@@ -86,24 +86,50 @@
     def shard(index):
         return pl.ds(pl.multiple_of(index * shard_rows, 16), shard_rows)
 
-    def next_copy(slot, index, peer):
+    z = r // 2
+
+    def next_copy(source, send_slot, recv_slot, peer):
+        rows = shard(source * 2 + r % 2)
         return pltpu.make_async_remote_copy(
-            src_ref=next_ref.at[shard(index)], dst_ref=next_ref.at[shard(index)],
-            send_sem=next_send.at[slot], recv_sem=next_recv.at[slot],
+            src_ref=next_ref.at[rows], dst_ref=next_ref.at[rows],
+            send_sem=next_send.at[send_slot], recv_sem=next_recv.at[recv_slot],
             device_id={"req": peer}, device_id_type=MESH,
         )
 
-    def z_copy(k):
-        return next_copy(k, r, (r + 2 * k) % senders)
-
-    def forward(k):
-        return next_copy(heights - 1 + k, (r + senders - 2 * k) % senders, x_peer)
-
-    def pass_on(k):
-        if gather:
-            z_copy(k).wait_recv()
-            forward(k).start()
-
+    def up(source):
+        return next_copy(source, source, source, (r + 2) % senders)
+
+    def down(source):
+        return next_copy(source, heights + source, source, (r + senders - 2) % senders)
+
+    def across(source):
+        return next_copy(source, 2 * heights + source, heights + source, x_peer)
+
+    def spread_up(source):
+        @pl.when(z < heights - 1)
+        def _():
+            up(source).start()
+
+    def spread_down(source):
+        @pl.when(z > 0)
+        def _():
+            down(source).start()
+
+    def pass_on(d):
+        if not gather:
+            return
+
+        @pl.when(z >= d)
+        def _():
+            up(z - d).wait_recv()
+            spread_up(z - d)
+            across(z - d).start()
+
+        @pl.when(z + d < heights)
+        def _():
+            down(z + d).wait_recv()
+            spread_down(z + d)
+            across(z + d).start()
 
     loads = [
         pltpu.make_async_copy(a, b, load_sem.at[i])
@@ -148,27 +174,16 @@
 
     if gather:
         loads[4].wait()
-        next_copy(0, r, x_peer).start()
-        for k in range(1, heights, 2):
-            z_copy(k).start()
+        spread_up(z)
+        spread_down(z)
+        across(z).start()
 
     loads[0].wait()
 
     def quadrant_step(step, c):
-        if gather:
-            @pl.when(step == 1)
-            def _():
-                for k in range(2, heights, 2):
-                    z_copy(k).start()
-
-            @pl.when(step == 2)
-            def _():
-                pass_on(1)
-
-            @pl.when(step == 3)
-            def _():
-                for k in range(3, heights, 2):
-                    pass_on(k)
+        @pl.when(step == 2)
+        def _():
+            pass_on(1)
 
         first = 1 - step // 2
         second = 1 - step % 2
@@ -223,6 +238,7 @@
         return c
 
     lax.fori_loop(0, lanes, quadrant_step, 0)
+    pass_on(2)
     counts_row = len_ref[...] // 4
     down_index = lax.broadcasted_iota(jnp.int32, (senders, senders), 0)
     across_index = lax.broadcasted_iota(jnp.int32, (senders, senders), 1)
@@ -278,7 +294,7 @@
         share_ref[y_peer].astype(jnp.float32) + share_in_ref[0].astype(jnp.float32)
     ).astype(jnp.bfloat16)
     share_y.start()
-    for k in range(2, heights, 2):
+    for k in range(3, heights):
         pass_on(k)
     shares[1].wait_recv()
     total = share_ref[m].astype(jnp.float32) + share_in_ref[1].astype(jnp.float32)
@@ -333,11 +349,8 @@
     row_y.start()
     row_core.start()
     if gather:
-        for k in range(heights):
-            if k:
-                forward(k).wait_recv()
-            else:
-                next_copy(0, r, x_peer).wait_recv()
+        for source in range(heights):
+            across(source).wait_recv()
     else:
         loads[4].wait()
     part = next_ref.shape[1] // 3
@@ -419,10 +432,16 @@
 
     lax.fori_loop(1, senders, drain, 0)
     if gather:
-        next_copy(0, r, x_peer).wait_send()
-        for k in range(1, heights):
-            z_copy(k).wait_send()
-            forward(k).wait_send()
+        for source in range(heights):
+            across(source).wait_send()
+
+            @pl.when((source <= z) & (z < heights - 1))
+            def _():
+                up(source).wait_send()
+
+            @pl.when((source >= z) & (z > 0))
+            def _():
+                down(source).wait_send()
 
 
 def front(places, marks, lengths, owners, residual_in, norm2_gain, norm2_bias, up_weight, up_bias,
@@ -479,7 +498,7 @@
             dma((lanes - 1,)), dma((lanes - 1,)),
             dma((senders - 1,)), dma((senders - 1,)),
             dma((3,)), dma((3,)),
-            dma((senders - 1,)), dma((senders - 1,)),
+            dma((3 * senders // 2,)), dma((senders,)),
             dma((lanes - 1,)), dma((lanes - 1,)),
         ],
         compiler_params=pltpu.CompilerParams(

time: 114 us -> 95.2 us (0.84)
  the two profiles are of different devices: /device:TPU:19 before, /device:TPU:0 now
where the time goes in v5:
time: 95.2 us; the launch traced here: 94.7 us
  Pallas kernels  84.5 us (89%)
  local copies, waits for them, and re-layouts  9.51 us (10%)
    pallas_call x1, Pallas kernels, front(): pl.pallas_call(functools.partial(front_kernel, (senders, slots, pad), gat...  84.5 us
    another operation x6, local copies, waits for them, and re-layouts, front(): jnp.stack([norm2_gain, norm2_bias, down_bias, norm3_gain, norm3_bias])  4.33 us
    unnamed x4, local copies, waits for them, and re-layouts  3.6 us

profile of v5, /device:TPU:0, one launch (start us, length us, event | category | flops | bytes accessed | tf_op | source)
XLA Modules:
  0.0 94.7 jit_solution(12245983004844919559)
XLA Ops:
  0.6 0.0 copy-start
  0.6 0.8 stack.18
  1.5 0.7 stack.19
  2.2 0.7 stack.20
  2.9 0.7 stack.21
  3.6 0.7 stack.22
  4.3 0.7 stack.23.params_ref
  5.0 0.0 copy-done
  5.0 0.3 constant_dynamic-slice_fusion
  5.3 0.3 copy.18
  5.6 1.0 %copy.19.next_hbm = bf16[208,1248]{1,0:T(8,128)(2,1)} copy(bf16[208,1248]{0,1:T(8,128)(2,1)S(1)} %bitcast.6) | data formatting | bytes 1038336 | tf_op jit(solution)/shard_map/reshape | solution.py:536
  6.6 84.5 %front.1 = (bf16[128,1664]{1,0:T(8,128)(2,1)}, bf16[128,1664]{1,0:T(8,128)(2,1)}) custom-call(s32[4,1,256]{2,1,0:T(1,128)} %bitcast.7, s32[4,1,256]{2,1,0:T(1,128)} %bitcast.8, s32[1,8]{1,0:T(1,128)} %bitcast.10, s32[1,8]{1,0:T(1,128)} %bitcast.11, f32[1,1024]{1,0:T(1,128)} %bitcast.9, f32[5,1664]{1,0:T(8,128)} %stack.23.params_ref, ...), custom_call_target="tpu_custom_call" | custom-call | flops 33587986432 | bytes 67108864 | tf_op jit(solution)/shard_map/front/pallas_call | solution.py:466
  91.1 1.8 %copy.22 = bf16[128,1664]{1,0:T(8,128)(2,1)} copy(bf16[128,1664]{1,0:T(8,128)(2,1)} %get-tuple-element.4) | data formatting | bytes 851968
  92.9 1.8 %copy.23 = bf16[128,1664]{1,0:T(8,128)(2,1)} copy(bf16[128,1664]{1,0:T(8,128)(2,1)} %get-tuple-element.5) | data formatting | bytes 851968
Async XLA Ops:
  0.6 4.4 %copy-start = (bf16[208,3,1664]{2,0,1:T(8,128)(2,1)S(1)}, bf16[208,3,1664]{2,0,1:T(8,128)(2,1)}, u32[]{:S(2)}) copy-start(bf16[208,3,1664]{2,0,1:T(8,128)(2,1)} %param.29) | copy-start | bytes 6230020

commit v6 on v5

--- a/solution.py
+++ b/solution.py
@@ -25,7 +25,11 @@
     len_ref,
     owner_ref,
     up_bias_ref,
-    params_ref,
+    gain2_ref,
+    bias2_ref,
+    down_bias_ref,
+    gain3_ref,
+    bias3_ref,
     residual_hbm,
     up_hbm,
     down_hbm,
@@ -154,6 +158,9 @@
     lax.fori_loop(1, senders, greet, 0)
     pl.semaphore_wait(barrier, lanes - 1 + senders - 1)
 
+    def row_of(ref):
+        return ref[...].reshape(1, width)
+
     def norm(values, gain, bias):
         mean_value = jnp.mean(values, axis=-1, keepdims=True)
         centred = values - mean_value
@@ -197,7 +204,7 @@
                 residual_ref[b * own_rows : (b + 1) * own_rows, :],
                 preferred_element_type=jnp.float32,
             )
-        normed = norm(xq_ref[...], params_ref[0:1, :], params_ref[1:2, :]).astype(jnp.bfloat16)
+        normed = norm(xq_ref[...], row_of(gain2_ref), row_of(bias2_ref)).astype(jnp.bfloat16)
 
         @pl.when(step == 0)
         def _():
@@ -266,7 +273,7 @@
     y_copy.wait_recv()
     layer_out = (
         xq_ref[...] + (acc_ref[...] + core_in_ref[1].astype(jnp.float32) + y_in_ref[...].astype(jnp.float32))
-        + params_ref[2:3, :]
+        + row_of(down_bias_ref)
     ).astype(jnp.bfloat16)
     loads[3].wait()
     acc_ref[...] = jnp.dot(layer_out, proj_ref[...], preferred_element_type=jnp.float32)
@@ -334,7 +341,7 @@
     merged_ref[...] = received
     everyone_ref[m, :, width:] = arrived[:, width:]
     everyone_ref[m, :, :width] = norm(
-        received.astype(jnp.float32), params_ref[3:4, :], params_ref[4:5, :]
+        received.astype(jnp.float32), row_of(gain3_ref), row_of(bias3_ref)
     ).astype(jnp.bfloat16)
 
     def row_copy(slot, block, peer):
@@ -458,7 +465,7 @@
     bf16, f32 = jnp.bfloat16, jnp.float32
     small = [
         places, marks, lengths.reshape(1, -1), owners.reshape(1, -1), up_bias.reshape(1, -1),
-        jnp.stack([norm2_gain, norm2_bias, down_bias, norm3_gain, norm3_bias]),
+        norm2_gain, norm2_bias, down_bias, norm3_gain, norm3_bias,
     ]
     large = [residual_in, up_weight, down_weight, proj_weight, next_part]
     dma = pltpu.SemaphoreType.DMA

time: 95.2 us -> 92.1 us (0.967)
  local copies, waits for them, and re-layouts: 9.51 us -> 6.75 us
    another operation x6 -> x0, local copies, waits for them, and re-layouts: 4.33 us -> none  [front(): jnp.stack([norm2_gain, norm2_bias, down_bias, norm3_gain, norm3_bias])]
    unnamed x4, local copies, waits for them, and re-layouts: 3.6 us -> 5.17 us
where the time goes in v6:
time: 92.1 us; the launch traced here: 91.9 us
  Pallas kernels  84.5 us (92%)
  local copies, waits for them, and re-layouts  6.75 us (7%)
    pallas_call x1, Pallas kernels, front(): pl.pallas_call(functools.partial(front_kernel, (senders, slots, pad), gat...  84.5 us
    unnamed x4, local copies, waits for them, and re-layouts  5.17 us

profile of v6, /device:TPU:0, one launch (start us, length us, event | category | flops | bytes accessed | tf_op | source)
XLA Modules:
  0.0 91.9 jit_solution(15252858142410862490)
XLA Ops:
  0.6 0.0 copy-start
  0.6 1.6 %copy-done = bf16[208,3,1664]{2,0,1:T(8,128)(2,1)S(1)} copy-done((bf16[208,3,1664]{2,0,1:T(8,128)(2,1)S(1)}, bf16[208,3,1664]{2,0,1:T(8,128)(2,1)}, u32[]{:S(2)}) %copy-start) | copy-done | bytes 2076696
  2.2 0.3 constant_dynamic-slice_fusion
  2.5 0.3 copy.18
  2.8 1.0 %copy.19.next_hbm = bf16[208,1248]{1,0:T(8,128)(2,1)} copy(bf16[208,1248]{0,1:T(8,128)(2,1)S(1)} %bitcast.6) | data formatting | bytes 1038336 | tf_op jit(solution)/shard_map/reshape | solution.py:543
  3.8 84.5 %front.1 = (bf16[128,1664]{1,0:T(8,128)(2,1)}, bf16[128,1664]{1,0:T(8,128)(2,1)}) custom-call(s32[4,1,256]{2,1,0:T(1,128)} %bitcast.7, s32[4,1,256]{2,1,0:T(1,128)} %bitcast.8, s32[1,8]{1,0:T(1,128)} %bitcast.10, s32[1,8]{1,0:T(1,128)} %bitcast.11, f32[1,1024]{1,0:T(1,128)} %bitcast.9, f32[1664]{0:T(1024)} %gain2_ref.1, f32[1664]{0:T(1024)} %bias2_ref.1, ...), custom_call_target="tpu_custom_call" | custom-call | flops 33587986432 | bytes 67108864 | tf_op jit(solution)/shard_map/front/pallas_call | solution.py:473
  88.3 1.8 %copy.22 = bf16[128,1664]{1,0:T(8,128)(2,1)} copy(bf16[128,1664]{1,0:T(8,128)(2,1)} %get-tuple-element.4) | data formatting | bytes 851968
  90.1 1.8 %copy.23 = bf16[128,1664]{1,0:T(8,128)(2,1)} copy(bf16[128,1664]{1,0:T(8,128)(2,1)} %get-tuple-element.5) | data formatting | bytes 851968
Async XLA Ops:
  0.6 1.6 %copy-start = (bf16[208,3,1664]{2,0,1:T(8,128)(2,1)S(1)}, bf16[208,3,1664]{2,0,1:T(8,128)(2,1)}, u32[]{:S(2)}) copy-start(bf16[208,3,1664]{2,0,1:T(8,128)(2,1)} %param.29) | copy-start | bytes 6230020
